TPU v7x, 32 devices: a whole 2x2x4 slice. The times are simulated.
32 devices in a mesh: ctx: 16 (over z, x, core), fsdp: 2 (over y).
Axes of the slice: x: 2, y: 2, z: 4, core: 2. Of those that a mesh axis runs over, the one named last changes fastest.
Arguments:
- tokens: bfloat16 [4096, 1152], P(('ctx', 'fsdp')), may hold values from -6 to 6
- query_weight: bfloat16 [1152, 1152], P('fsdp'), may hold values from -0.4375 to 0.4375
- key_projection: bfloat16 [1152, 384], P('fsdp'), may hold values from -0.1875 to 0.1875
- value_projection: bfloat16 [1152, 384], P('fsdp'), may hold values from -0.1875 to 0.1875
- output_weight: bfloat16 [1152, 1152], P('fsdp'), may hold values from -1 to 1
- gate_weight: bfloat16 [1152, 3072], P('fsdp'), may hold values from -0.1875 to 0.1875
- up_weight: bfloat16 [1152, 3072], P('fsdp'), may hold values from -0.1875 to 0.1875
- down_weight: bfloat16 [3072, 1152], P('fsdp'), may hold values from -0.109375 to 0.109375
- norm_attn: bfloat16 [1152], P('fsdp'), may hold values from 0.5 to 1.5
- norm_mlp: bfloat16 [1152], P('fsdp'), may hold values from 0.5 to 1.5
- doc_starts: int32 [4], replicated, may hold values from 0 to 4095, as said below
- cotangent: bfloat16 [4096, 1152], P(('ctx', 'fsdp')), may hold values from -6 to 6
Outputs:
- result: bfloat16 [4096, 1152], P(('ctx', 'fsdp'))
- tokens_grad: float32 [4096, 1152], P(('ctx', 'fsdp'))
- query_grad: float32 [1152, 1152], P('fsdp', 'ctx')
- key_grad: float32 [1152, 384], P('fsdp', 'ctx')
- value_grad: float32 [1152, 384], P('fsdp', 'ctx')
- output_grad: float32 [1152, 1152], P('fsdp', 'ctx')
- gate_grad: float32 [1152, 3072], P('fsdp', 'ctx')
- up_grad: float32 [1152, 3072], P('fsdp', 'ctx')
- down_grad: float32 [3072, 1152], P('fsdp', 'ctx')
- norm_attn_grad: float32 [1152], replicated
- norm_mlp_grad: float32 [1152], replicated
Inputs may be any that keep to these rules, and one draw needn't show every extreme that they name: `doc_starts`: strictly increasing positions where documents begin, the first 0 and the last 4095; the second is one of positions 1 to 64 and the third one of positions 4032 to 4094, so one document runs from the first device's tokens to the last device's.
All inputs are finite; a program needn't handle non-finite values.
Results may differ from a plain program's by a relative error of at most 0.02.
Values may be sent and summed in bfloat16 or wider, within the bound.
A program may use at most 384 MiB of HBM per device.

v0:
```python
import functools
import math

import jax
import jax.numpy as jnp
from jax import lax
from jax.experimental import pallas as pl
from jax.experimental.pallas import tpu as pltpu
from jax.sharding import PartitionSpec as P

QUERY_HEADS = 18
KEY_VALUE_HEADS = 6
HEAD_SIZE = 64
HS = HEAD_SIZE

EPS = 1e-05
THETA = 10000.0
NEG = -1e30
AXES = ("ctx", "fsdp")


def rope_tables(positions):
    half_dim = HEAD_SIZE // 2
    frequency = jnp.exp(-math.log(THETA) * jnp.arange(half_dim, dtype=jnp.float32) / half_dim)
    angles = positions.astype(jnp.float32)[:, None] * frequency[None, :]
    return (jnp.cos(angles), jnp.sin(angles))


def apply_rotary(values, cosine_table, sine_table):
    half_dim = values.shape[-1] // 2
    first_half = values[..., :half_dim]
    second_half = values[..., half_dim:]
    cos_rows = cosine_table[:, None, :]
    sin_rows = sine_table[:, None, :]
    return jnp.concatenate(
        [
            first_half * cos_rows - second_half * sin_rows,
            second_half * cos_rows + first_half * sin_rows,
        ],
        axis=-1,
    )


def unrotate(values, cosine_table, sine_table):
    half_dim = values.shape[-1] // 2
    first_half = values[..., :half_dim]
    second_half = values[..., half_dim:]
    cos_rows = cosine_table[:, None, :]
    sin_rows = sine_table[:, None, :]
    return jnp.concatenate(
        [
            first_half * cos_rows + second_half * sin_rows,
            second_half * cos_rows - first_half * sin_rows,
        ],
        axis=-1,
    )


def doc_begin(indices, doc_starts):
    marked = jnp.where(indices[:, None] >= doc_starts[None, :], doc_starts[None, :], 0)
    return jnp.max(marked, axis=1)


def layout_rows(device, row_count):
    return device * row_count + jnp.arange(row_count, dtype=jnp.int32)


def heads_rows(natural):
    return jnp.transpose(natural.astype(jnp.float32))
def padded(rows, heads, g):
    top = jnp.concatenate([rows[HS*(heads*g+j):HS*(heads*g+j+1)] for j in range(heads)], axis=1)
    z = jnp.zeros_like(top)
    return jnp.concatenate([top, z] if g == 0 else [z, top], axis=0)
def head_lanes(per_group, heads, tq):
    return jnp.transpose(jnp.concatenate([per_group[g][:, tq*j:tq*(j+1)] for g in range(2) for j in range(heads)], axis=0))
def bias_tile(info, docs, first, bk, tq):
    query = info[0] + lax.broadcasted_iota(jnp.int32, (1, tq), 1)
    begin = jnp.zeros((1, tq), jnp.int32)
    for i in range(docs.shape[0]):
        begin = jnp.maximum(begin, jnp.where(query >= docs[i], docs[i], 0))
    key = first + lax.broadcasted_iota(jnp.int32, (bk, 1), 0)
    return jnp.where((key <= query) & (key >= begin), 0.0, NEG)


def line_dims(count):
    fours = 0
    while count % 4 == 0:
        count //= 4
        fours += 1
    return ([count] if count > 1 else []) + [4] * fours


def rotate_back(rows, cos_rows, sin_rows):
    half_dim = HS // 2
    first, second = rows[:half_dim], rows[half_dim:]
    return jnp.concatenate(
        [first * cos_rows + second * sin_rows, second * cos_rows - first * sin_rows], axis=0
    )


def w_order(lines):
    return [lines[-2]] + lines[1:-2] + [lines[0], lines[-1]]


def bit_dims(count):
    return [2] * (count.bit_length() - 1)


def round_up(value, unit):
    return -(-value // unit) * unit


def backward_kernel(plan, docs, q_ref, do_ref, ot_ref, lse_ref, kv_hbm, w_ref, cos_ref, sin_ref,
                    normed_ref, inv_ref, gain_ref, gres_ref, gmlp_ref, low_ref, branch_ref, gup_hbm, dnp_hbm, inputs_hbm,
                    tokens_ref, query_ref, key_ref, value_ref, gains_out, gate_ref, up_ref, down_ref, out_ref,
                    kvbuf, dkv, acc_ref, gqt_ref, ga_ref, qblk, kvblk, small,
                    load_sem, send_sem, recv_sem, col_send, col_recv, own_sem, credit,
                    wg, wd, wo, brs, lows, halves, fin, fin_in, dsend, din,
                    colq_ref, colkv_ref, gains_ref, cols_acc, half_send, half_in, gain_send, gain_in, in_sem,
                    g_send, g_recv, w_load, w_send, w_recv, top_send, top_recv, fin_send, fin_recv, *recvs):
    nctx, nf, parts, heads, tq, slots = plan
    plane = nctx // 2
    n = nctx * nf
    dims = bit_dims(plane)
    nd = len(dims)
    bk = 2 * nf * tq
    me_c, me_f = lax.axis_index("ctx"), lax.axis_index("fsdp")
    me = me_c * nf + me_f
    core, place = lax.rem(me_c, 2), me_c // 2
    mesh_id = pl.DeviceIdType.MESH
    half_dim = HS // 2

    def target(k):
        other = lax.rem(me + k, n)
        return other, {"ctx": other // nf, "fsdp": lax.rem(other, nf)}

    barrier = pltpu.get_barrier_semaphore()

    def greet(k, carry):
        pl.semaphore_signal(barrier, inc=1, device_id=target(k)[1], device_id_type=mesh_id)
        return carry

    lax.fori_loop(1, n, greet, 0)

    def loads(p):
        s = p % slots
        return [
            pltpu.make_async_copy(
                kv_hbm.at[:, pl.ds((kind * parts + p) * 2 * HS, 2 * HS)],
                kvbuf.at[s, kind], load_sem.at[s, kind],
            )
            for kind in range(2)
        ]

    resident = slots == parts

    def block_loads(p, j):
        slot = lax.rem(j, 2)
        return [
            pltpu.make_async_copy(
                kv_hbm.at[pl.ds(pl.multiple_of(j * bk, bk), bk), pl.ds((kind * parts + p) * 2 * HS, 2 * HS)],
                kvbuf.at[slot, kind], load_sem.at[slot, kind],
            )
            for kind in range(2)
        ]

    if resident:
        for p in range(parts):
            for copy in loads(p):
                copy.start()

    def dim_axis(i):
        stride = math.prod(dims[:i])
        size = dims[i]
        own = lax.rem(place // stride, size)

        def peer(k):
            there = lax.rem(own + k, size)
            return there, {"ctx": (place + (there - own) * stride) * 2 + core, "fsdp": me_f}

        return (nd - 1 - i, size, own, peer)

    core_axis = (nd, 2, core, lambda k: (1 - core, {"ctx": place * 2 + 1 - core, "fsdp": me_f}))
    side_axis = (nd + 1, 2, me_f, lambda k: (1 - me_f, {"ctx": me_c, "fsdp": 1 - me_f}))
    lines = [dim_axis(i) for i in range(nd)]
    orders = [[core_axis, side_axis] + lines, [core_axis, lines[0], side_axis] + lines[1:]]
    stages = nd + 2
    wrecvs = recvs[2 * stages :]
    side_at, mate_at = side_axis[3](1)[1], core_axis[3](1)[1]

    low_bits = nd - 2
    arrays = ((wg, gup_hbm), (wd, dnp_hbm), (wo, None))
    w_lines = [lines, w_order(lines), lines]

    def chunk_at(a, k):
        near, far_line = w_lines[a][nd - 2], w_lines[a][nd - 1]
        far_bit = far_line[2] if k % 2 else 1 - far_line[2]
        near_bit = near[2] if k // 2 else 1 - near[2]
        return far_bit, near_bit

    def w_region(a, k, stage, at):
        index = [slice(None)] * nd
        index[w_lines[a][nd - 1][0]], index[w_lines[a][nd - 2][0]] = chunk_at(a, k)
        for axis in w_lines[a][:stage]:
            index[axis[0]] = axis[2]
        if stage < low_bits:
            index[w_lines[a][stage][0]] = at
        return tuple(index)

    def held(a, index):
        first = w_lines[a][0][0]
        return index if a == 2 else index[:first] + index[first + 1 :]

    def w_copy(a, k, stage):
        buf, far = arrays[a]
        there, where = w_lines[a][stage][3](1)
        index = w_region(a, k, stage, there)
        return pltpu.make_async_remote_copy(
            src_ref=far.at[index] if stage == 0 and a < 2 else buf.at[held(a, index)],
            dst_ref=wrecvs[a * (low_bits + 2) + stage].at[chunk_at(a, k)],
            send_sem=w_send.at[a, k, stage], recv_sem=w_recv.at[a, k, stage],
            device_id=where, device_id_type=mesh_id,
        )

    def near_copy(a, i):
        return pltpu.make_async_remote_copy(
            src_ref=arrays[a][0].at[held(a, w_region(a, i, low_bits, 0))], dst_ref=wrecvs[a * (low_bits + 2) + low_bits].at[i],
            send_sem=top_send.at[a, i], recv_sem=top_recv.at[a, i],
            device_id=w_lines[a][nd - 2][3](1)[1], device_id_type=mesh_id,
        )

    def far_copy(a):
        return pltpu.make_async_remote_copy(
            src_ref=arrays[a][0].at[held(a, w_region(a, 2, low_bits, 0))], dst_ref=wrecvs[a * (low_bits + 2) + low_bits + 1].at[0],
            send_sem=top_send.at[a, 2], recv_sem=top_recv.at[a, 2],
            device_id=w_lines[a][nd - 1][3](1)[1], device_id_type=mesh_id,
        )

    def w_start(which, k):
        for a in which:
            w_copy(a, k, 0).start()

    def w_finish(which, k):
        for a in which:
            buf = arrays[a][0]
            for stage in range(low_bits):
                w_copy(a, k, stage).wait()
                where = held(a, w_region(a, k, stage, w_lines[a][stage][2]))
                got = wrecvs[a * (low_bits + 2) + stage]
                buf[where] = (
                    buf[where].astype(jnp.float32) + got[chunk_at(a, k)].astype(jnp.float32)
                ).astype(buf.dtype)
                if stage + 1 < low_bits:
                    w_copy(a, k, stage + 1).start()
            if k < 2:
                near_copy(a, k).start()
            elif k == 2:
                near_copy(a, 0).wait()
                where = held(a, w_region(a, 2, low_bits, 0))
                buf[where] = (
                    buf[where].astype(jnp.float32)
                    + wrecvs[a * (low_bits + 2) + low_bits][0].astype(jnp.float32)
                ).astype(buf.dtype)
                far_copy(a).start()

    def w_total(a):
        near_copy(a, 1).wait()
        far_copy(a).wait()
        total = arrays[a][0][held(a, w_region(a, 3, low_bits, 0))].astype(jnp.float32)
        total = total + wrecvs[a * (low_bits + 2) + low_bits][1].astype(jnp.float32)
        return total + wrecvs[a * (low_bits + 2) + low_bits + 1][0].astype(jnp.float32)

    w_loads = [
        pltpu.make_async_copy(far.at[(slice(None),) * w_lines[i][0][0] + (w_lines[i][0][2],)], buf, w_load.at[i])
        for i, (buf, far) in enumerate(arrays[:2])
    ]
    for copy in w_loads:
        copy.start()
    half = low_ref.shape[1] // nf
    low_all = low_ref[...]
    halves[0] = low_all[:, :half]
    halves[1] = low_all[:, half:]
    lows[0] = halves[me_f]
    brs[0] = branch_ref[...]

    def g_copy(i, src, dst, where):
        return pltpu.make_async_remote_copy(
            src_ref=src, dst_ref=dst, send_sem=g_send.at[i], recv_sem=g_recv.at[i],
            device_id=where, device_id_type=mesh_id,
        )

    low_side = g_copy(0, halves.at[1 - me_f], lows.at[1], side_at)
    br_side = g_copy(1, brs.at[0], brs.at[1], side_at)
    low_core = g_copy(2, lows.at[pl.ds(0, 2)], lows.at[pl.ds(2, 2)], mate_at)
    br_core = g_copy(3, brs.at[pl.ds(0, 2)], brs.at[pl.ds(2, 2)], mate_at)

    def output_partial():
        low_core.wait()
        br_core.wait()
        rows = jnp.transpose(brs[...].reshape(4 * tq, brs.shape[2]))
        unit = brs.shape[2] // nctx
        wo[...] = jnp.zeros_like(wo)
        low_rows = lows[...].reshape(4 * tq, half)
        batch = plane // 4
        for r in range(plane):
            first = 2 * unit * (r % batch)
            if first == 0:
                chunk = 2 * unit * batch
                part = jnp.dot(
                    rows[2 * unit * r : 2 * unit * r + chunk], low_rows, preferred_element_type=jnp.float32
                )
            piece = jnp.where(core == 0, part[first : first + unit], part[first + unit : first + 2 * unit])
            wo[static_index(dims, r) + (slice(0, unit), slice(0, half))] = piece.astype(wo.dtype)

    pl.semaphore_wait(barrier, n - 1)
    low_side.start()
    br_side.start()
    w_start((0, 1), 0)
    w_start((0, 1), 1)

    def region(kind, stage, at):
        index = [slice(None)] * (nd + 2)
        for axis in orders[kind][:stage]:
            index[axis[0]] = axis[2]
        index[orders[kind][stage][0]] = at
        return tuple(index)

    def stage_copies(p, kind, stage):
        s = p % slots
        axis = orders[kind][stage]
        copies = []
        for k in range(1, axis[1]):
            there, where = axis[3](k)
            copies.append(
                pltpu.make_async_remote_copy(
                    src_ref=dkv.at[(s, kind) + region(kind, stage, there)],
                    dst_ref=recvs[kind * stages + stage].at[s, k - 1],
                    send_sem=send_sem.at[s, kind, stage, k - 1],
                    recv_sem=recv_sem.at[s, kind, stage, k - 1],
                    device_id=where, device_id_type=mesh_id,
                )
            )
        return copies

    def stage_start(p, stage):
        for kind in range(2):
            for copy in stage_copies(p, kind, stage):
                copy.start()

    finals = {}

    def stage_finish(p, stage):
        s = p % slots
        for kind in range(2):
            axis = orders[kind][stage]
            for copy in stage_copies(p, kind, stage):
                copy.wait()
            where = region(kind, stage, axis[2])
            got = recvs[kind * stages + stage]
            free = [i for i in range(nd + 2) if isinstance(where[i], slice)]

            def add(index, lead):
                total = dkv[(s, kind) + index].astype(jnp.float32)
                for k in range(axis[1] - 1):
                    total = total + got[(s, k) + lead].astype(jnp.float32)
                return total

            if not free:
                finals[p, kind] = add(where, ())
            else:
                size = dkv.shape[2 + free[0]]

                def one(i, carry):
                    index = list(where)
                    index[free[0]] = i
                    index = tuple(index)
                    dkv[(s, kind) + index] = add(index, (i,)).astype(dkv.dtype)
                    return carry

                lax.fori_loop(0, size, one, 0)

    def place_index(j):
        index = []
        for i in reversed(range(nd)):
            index.append(lax.rem(j // math.prod(dims[:i]), dims[i]))
        return tuple(index)

    start = me * tq
    last = (start + tq - 1) // bk + 1

    def compute(p):
        s = p % slots
        span = slice(2 * heads * HS * p, 2 * heads * HS * (p + 1))
        qt = q_ref[span, :].astype(jnp.float32) * (1.0 / 8.0)
        dt = heads_rows(do_ref[:, span])
        qg = [padded(qt, heads, g) for g in range(2)]
        dg = [padded(dt, heads, g) for g in range(2)]
        qrows = jnp.concatenate([jnp.transpose(x) for x in qg], axis=0).astype(jnp.bfloat16)
        drows = jnp.concatenate([jnp.transpose(x) for x in dg], axis=0).astype(jnp.bfloat16)
        delta = [
            jnp.sum(dg[g][HS * g : HS * (g + 1)] * ot_ref[2 * p + g], axis=0, keepdims=True)
            for g in range(2)
        ]
        lse = [lse_ref[2 * p + g] for g in range(2)]
        qg = [x.astype(jnp.bfloat16) for x in qg]
        dg = [x.astype(jnp.bfloat16) for x in dg]
        acc_ref[...] = jnp.zeros_like(acc_ref)
        for copy in loads(p) if resident else block_loads(p, 0):
            if not resident:
                copy.start()
            else:
                copy.wait()

        def zero(j, carry):
            at = place_index(j)
            for kind in range(2):
                dkv[(s, kind) + at] = jnp.zeros((2, nf, tq, 2 * HS), dkv.dtype)
            return carry

        def body(j, carry):
            first = pl.multiple_of(j * bk, bk)
            if resident:
                kb = kvbuf[s, 0, pl.ds(first, bk), :]
                vb = kvbuf[s, 1, pl.ds(first, bk), :]
            else:
                for copy in block_loads(p, j):
                    copy.wait()

                @pl.when(j + 1 < last)
                def _():
                    for copy in block_loads(p, j + 1):
                        copy.start()

                kb, vb = kvbuf[lax.rem(j, 2), 0], kvbuf[lax.rem(j, 2), 1]
            kt = jnp.transpose(kb)
            bias = bias_tile((start,), docs, first, bk, tq)
            bias = jnp.concatenate([bias] * heads, axis=1)
            ps = []
            dss = []
            for g in range(2):
                score = jnp.dot(kb, qg[g], preferred_element_type=jnp.float32)
                prob = jnp.exp(score + (bias - lse[g]))
                dp = jnp.dot(vb, dg[g], preferred_element_type=jnp.float32)
                ds = (prob * (dp - delta[g])).astype(jnp.bfloat16)
                ps.append(prob.astype(jnp.bfloat16))
                dss.append(ds)
                acc_ref[g] += jnp.dot(kt[HS * g : HS * (g + 1)], ds, preferred_element_type=jnp.float32)
            dv = jnp.dot(jnp.concatenate(ps, axis=1), drows, preferred_element_type=jnp.float32)
            dk = jnp.dot(jnp.concatenate(dss, axis=1), qrows, preferred_element_type=jnp.float32)
            at = place_index(j)
            dkv[(s, 0) + at] = dk.astype(dkv.dtype).reshape(2, nf, tq, 2 * HS)
            dkv[(s, 1) + at] = dv.astype(dkv.dtype).reshape(2, nf, tq, 2 * HS)
            return carry

        lax.fori_loop(last, plane, zero, 0)
        lax.fori_loop(0, last, body, 0)
        cos_rows = jnp.concatenate([cos_ref[...]] * heads, axis=1) * (1.0 / 8.0)
        sin_rows = jnp.concatenate([sin_ref[...]] * heads, axis=1) * (1.0 / 8.0)
        for g in range(2):
            back = rotate_back(acc_ref[g], cos_rows, sin_rows).astype(gqt_ref.dtype)
            for j in range(heads):
                h = (2 * p + g) * heads + j
                gqt_ref[HS * h : HS * (h + 1), :] = back[:, tq * j : tq * (j + 1)]

    peers = 2 + sum(size - 1 for size in dims)

    def all_peers():
        found = [core_axis[3](1)[1], side_axis[3](1)[1]]
        for axis in lines:
            found += [axis[3](k)[1] for k in range(1, axis[1])]
        return found

    progress = {}

    def advance(p):
        stage = progress[p]
        stage_finish(p, stage)
        progress[p] = stage + 1
        if stage + 1 < stages:
            stage_start(p, stage + 1)
        else:
            del progress[p]
            if p + slots < parts:
                for where in all_peers():
                    pl.semaphore_signal(credit, inc=1, device_id=where, device_id_type=mesh_id)

    for p in range(parts):
        if p >= slots:
            while p - slots in progress:
                advance(p - slots)
        compute(p)
        if p >= slots:
            pl.semaphore_wait(credit, peers)
        stage_start(p, 0)
        progress[p] = 0
        for older in [o for o in progress if o < p]:
            advance(older)
        if p == 0:
            low_side.wait()
            br_side.wait()
            low_core.start()
            br_core.start()
        if p == 1:
            for copy in w_loads:
                copy.wait()
            w_finish((0, 1), 0)
            w_start((0, 1), 2)
            output_partial()
            for k in range(4):
                w_start((2,), k)
    w_finish((0, 1), 1)
    w_start((0, 1), 3)

    def copies_to(k, which):
        other = lax.rem(me_c + k, nctx)
        where = {"ctx": other, "fsdp": me_f}
        block, out = ((qblk, colq_ref), (kvblk, colkv_ref), (small, gains_ref))[which]
        return pltpu.make_async_remote_copy(
            src_ref=block if which == 2 else block.at[other], dst_ref=out.at[me_c],
            send_sem=col_send.at[which, k], recv_sem=col_recv.at[which, k],
            device_id=where, device_id_type=mesh_id,
        )

    def share(which):
        def one(k, carry):
            copies_to(k, which).start()
            return carry

        block, out = ((qblk, colq_ref), (kvblk, colkv_ref), (small, gains_ref))[which]
        pltpu.make_async_copy(block if which == 2 else block.at[me_c], out.at[me_c], own_sem.at[which]).start()
        lax.fori_loop(1, nctx, one, 0)

    def share_wait(which):
        def one(k, carry):
            copies_to(k, which).wait()
            return carry

        block, out = ((qblk, colq_ref), (kvblk, colkv_ref), (small, gains_ref))[which]
        pltpu.make_async_copy(block if which == 2 else block.at[me_c], out.at[me_c], own_sem.at[which]).wait()
        lax.fori_loop(1, nctx, one, 0)

    width_q = 2 * parts * heads * HS
    width_k = 2 * parts * HS
    cq, ck = width_q // nctx, width_k // nctx
    qblk[...] = jnp.zeros_like(qblk)
    kvblk[...] = jnp.zeros_like(kvblk)
    for i in range(nctx):
        qblk[i, 0:cq, :] = gqt_ref[cq * i : cq * (i + 1), :]
    share(0)
    ga_ref[...] = jnp.dot(w_ref[:, :width_q], gqt_ref[...], preferred_element_type=jnp.float32)
    for k in range(2):
        w_finish((2,), k)
    pq, pk = qblk.shape[1], kvblk.shape[1]

    def columns(col_ref, first, count):
        def fetch(i, slot):
            return pltpu.make_async_copy(
                inputs_hbm.at[i], brs.at[slot], in_sem.at[slot]
            )

        fetch(0, 0).start()
        cols_acc[first : first + count, :] = jnp.zeros((count, cols_acc.shape[1]), jnp.float32)

        def one(i, carry):
            slot = lax.rem(i, 2)

            @pl.when(i + 1 < nctx)
            def _():
                fetch(i + 1, 1 - slot).start()

            fetch(i, slot).wait()
            cols_acc[first : first + count, :] += jnp.dot(
                col_ref[i], brs[slot], preferred_element_type=jnp.float32
            )
            return carry

        lax.fori_loop(0, nctx, one, 0)

    turn = 0
    while progress:
        for p in list(progress):
            advance(p)
        if turn == 0:
            w_finish((0, 1, 2), 2)
        if turn == 1:
            w_finish((0, 1, 2), 3)
            share_wait(0)
            columns(colq_ref, 0, pq)
        turn += 1

    cos_rows, sin_rows = cos_ref[...], sin_ref[...]
    grads = []
    for kind in range(2):
        rows = []
        for p in range(parts):
            both = jnp.transpose(finals[p, kind])
            for g in range(2):
                one = both[HS * g : HS * (g + 1)]
                rows.append(rotate_back(one, cos_rows, sin_rows) if kind == 0 else one)
        grads.append(jnp.concatenate(rows, axis=0).astype(jnp.bfloat16))
    for i in range(nctx):
        kvblk[i, 0:ck, :] = grads[0][ck * i : ck * (i + 1)]
        kvblk[i, ck : 2 * ck, :] = grads[1][ck * i : ck * (i + 1)]
    share(1)
    grad_t = (
        ga_ref[...]
        + jnp.dot(w_ref[:, width_q : width_q + width_k], grads[0], preferred_element_type=jnp.float32)
        + jnp.dot(w_ref[:, width_q + width_k :], grads[1], preferred_element_type=jnp.float32)
    )
    grad = jnp.transpose(grad_t)
    normed = normed_ref[...].astype(jnp.float32) * inv_ref[...]
    product = grad * normed
    gain_sum = jnp.sum(product, axis=0, keepdims=True)
    lanes = 128
    tiles = gain_sum.shape[1] // lanes
    rows = [gain_sum[:, lanes * i : lanes * (i + 1)] for i in range(tiles)]
    rows += [gmlp_ref[:, lanes * i : lanes * (i + 1)] for i in range(tiles)]
    rows += [jnp.zeros((small.shape[0] - 2 * tiles, lanes), jnp.float32)]
    small[...] = jnp.concatenate(rows, axis=0)
    share(2)
    gain = gain_ref[0:1, :]
    scaled = grad * gain
    mean = jnp.mean(scaled * normed, axis=1, keepdims=True)
    tokens_ref[...] = gres_ref[...] + inv_ref[...] * (scaled - normed * mean)

    total = w_total(0)
    unit, lanes = fin.shape[2], fin.shape[3]
    blank = jnp.zeros((2, unit, lanes - half), fin.dtype)
    for s in range(2):
        fin[s] = jnp.concatenate([total[:, :, half * s : half * (s + 1)].astype(fin.dtype), blank], axis=2)
    dsum = w_total(1)
    dsend[...] = dsum.astype(dsend.dtype)
    down_copy = g_copy(4, dsend, din, mate_at)
    down_copy.start()
    per_side = plane // 2
    home = (2 * me_f + core) * per_side + place // 2
    slot = lax.rem(place, 2)

    def home_copy(s):
        return pltpu.make_async_remote_copy(
            src_ref=fin.at[s], dst_ref=fin_in.at[slot], send_sem=fin_send.at[s], recv_sem=fin_recv.at[slot],
            device_id={"ctx": home, "fsdp": jnp.int32(s)}, device_id_type=mesh_id,
        )

    def self_copy(s):
        return pltpu.make_async_copy(fin.at[s], fin_in.at[slot], fin_send.at[s])

    for s in range(2):
        at_home = (home == me_c) & (me_f == s)

        @pl.when(jnp.logical_not(at_home))
        def _():
            home_copy(s).start()

        @pl.when(at_home)
        def _():
            self_copy(s).start()

    osum = w_total(2)
    out_ref[...] = osum[: out_ref.shape[0], :half]
    share_wait(1)
    columns(colkv_ref, pq, pk)
    left, right = cols_acc[:, :half], cols_acc[:, half:]
    side_pad = jnp.zeros((pq + pk, half_send.shape[1] - half), half_send.dtype)
    half_send[...] = jnp.concatenate([jnp.where(me_f == 0, right, left).astype(half_send.dtype), side_pad], axis=1)
    half_copy = g_copy(5, half_send, half_in, side_at)
    half_copy.start()
    share_wait(2)
    gain_total = gains_ref[0]
    for i in range(1, nctx):
        gain_total = gain_total + gains_ref[i]
    gain_send[...] = gain_total
    gain_copy = g_copy(6, gain_send, gain_in, side_at)
    gain_copy.start()
    half_copy.wait()
    own_half = jnp.where(me_f == 0, cols_acc[:, :half], cols_acc[:, half:])
    rows = own_half + half_in[:, :half].astype(jnp.float32)
    query_ref[...] = rows[:cq]
    key_ref[...] = rows[pq : pq + ck]
    value_ref[...] = rows[pq + ck : pq + 2 * ck]
    gain_copy.wait()
    gains_out[...] = gain_send[...] + gain_in[...]
    down_copy.wait()
    cols = down_ref.shape[0]

    def unfold(folded):
        return jnp.concatenate(
            [folded[2 * cols * i : 2 * cols * (i + 1)] for i in range(folded.shape[0] // (2 * cols))], axis=1
        )

    dsum, got = unfold(dsum), unfold(din[...].astype(jnp.float32))
    own_cols = jnp.where(core == 0, dsum[:cols], dsum[cols:])
    far_cols = jnp.where(core == 0, got[:cols], got[cols:])
    down_ref[...] = jnp.where(
        core == 0,
        jnp.concatenate([own_cols, far_cols], axis=1),
        jnp.concatenate([far_cols, own_cols], axis=1),
    )
    for s in range(2):
        at_home = (home == me_c) & (me_f == s)

        @pl.when(jnp.logical_not(at_home))
        def _():
            home_copy(s).wait_send()

        @pl.when(at_home)
        def _():
            self_copy(s).wait()

    owner = me_c // per_side
    for h in range(2):
        holder = (2 * lax.rem(me_c, per_side) + h) * 2 + lax.rem(owner, 2)

        @pl.when(jnp.logical_not((holder == me_c) & (owner // 2 == me_f)))
        def _():
            pltpu.make_async_remote_copy(
                src_ref=fin.at[0], dst_ref=fin_in.at[h], send_sem=fin_send.at[0], recv_sem=fin_recv.at[h],
                device_id={"ctx": home, "fsdp": me_f}, device_id_type=mesh_id,
            ).wait_recv()

    for kind, ref in ((0, gate_ref), (1, up_ref)):
        rows = jnp.concatenate([fin_in[0, kind], fin_in[1, kind]], axis=0).astype(jnp.float32)
        ref[...] = rows[:, :half]


def backward(nctx, nf, docs, q, do, ot, lse, kv, w, cos_t, sin_t, normed, inv, gain, gres, gmlp, low, branch, gup, dnp, inputs):
    width_q, tq = q.shape
    n_tokens, width_kv = kv.shape
    n = nctx * nf
    parts = width_kv // (4 * HS)
    heads = width_q // HS // (2 * parts)
    dims = bit_dims(nctx // 2)
    lead = tuple(reversed(dims))
    part_bytes = n_tokens * 2 * HS * 2
    slots = parts if parts * part_bytes * 5 <= 24 * 2**20 else 1
    nd = len(dims)
    bf16, f32 = jnp.bfloat16, jnp.float32
    axes = {"core": (nd, 2), "side": (nd + 1, nf)}
    line = [(nd - 1 - i, dims[i]) for i in range(nd)]
    orders = [
        [axes["core"], axes["side"]] + line,
        [axes["core"], line[0], axes["side"]] + line[1:],
    ]
    recvs = []
    for order in orders:
        left = list(lead) + [2, nf]
        for position, size in order:
            left[position] = None
            recvs.append(
                pltpu.VMEM((slots, size - 1) + tuple(x for x in left if x) + (tq, 2 * HS), bf16)
            )
    model_width = low.shape[1]
    half = model_width // nf
    unit, deep = gup.shape[-2], model_width // (nctx // 2)
    quarter = dnp.shape[-2] // deep * 128
    plane = nctx // 2
    tails = [gup.shape[nd:], dnp.shape[nd:], (round_up(deep // 2, 16), round_up(half, 128))]
    for tail in tails:
        for stage in range(nd - 2):
            recvs.append(pltpu.VMEM((2,) * (nd - 1 - stage) + tail, bf16))
        recvs += [pltpu.VMEM((2,) + tail, bf16), pltpu.VMEM((1,) + tail, bf16)]
    stages = nd + 2
    most = max(dims + [2])
    pq = round_up(width_q // nctx, 16)
    pk = round_up(2 * (2 * parts * HS) // nctx, 16)
    model = w.shape[0]
    sr = round_up(2 * model // 128, 8)
    vmem = pl.BlockSpec(memory_space=pltpu.VMEM)
    smem = pl.BlockSpec(memory_space=pltpu.SMEM)
    hbm = pl.BlockSpec(memory_space=pl.ANY)
    return pl.pallas_call(
        functools.partial(backward_kernel, (nctx, nf, parts, heads, tq, slots)),
        out_shape=[
            jax.ShapeDtypeStruct((tq, model), f32),
            jax.ShapeDtypeStruct((width_q // nctx, half), f32),
            jax.ShapeDtypeStruct((2 * parts * HS // nctx, half), f32),
            jax.ShapeDtypeStruct((2 * parts * HS // nctx, half), f32),
            jax.ShapeDtypeStruct((sr, 128), f32),
            jax.ShapeDtypeStruct((2 * unit, half), f32),
            jax.ShapeDtypeStruct((2 * unit, half), f32),
            jax.ShapeDtypeStruct((deep // 2, 2 * quarter), f32),
            jax.ShapeDtypeStruct((deep // 2, half), f32),
        ],
        in_specs=[smem, vmem, vmem, vmem, vmem, hbm] + [vmem] * 10 + [hbm] * 3,
        out_specs=[vmem] * 9,
        scratch_shapes=[
            pltpu.VMEM((slots, 2, n_tokens, 2 * HS) if slots == parts else (2, 2, 2 * nf * tq, 2 * HS), bf16),
            pltpu.VMEM((slots, 2) + lead + (2, nf, tq, 2 * HS), bf16),
            pltpu.VMEM((2, HS, heads * tq), f32),
            pltpu.VMEM((width_q, tq), bf16),
            pltpu.VMEM((model, tq), f32),
            pltpu.VMEM((nctx, pq, tq), bf16),
            pltpu.VMEM((nctx, pk, tq), bf16),
            pltpu.VMEM((sr, 128), f32),
            pltpu.SemaphoreType.DMA((max(slots, 2), 2)),
            pltpu.SemaphoreType.DMA((slots, 2, stages, most - 1)),
            pltpu.SemaphoreType.DMA((slots, 2, stages, most - 1)),
            pltpu.SemaphoreType.DMA((3, nctx)),
            pltpu.SemaphoreType.DMA((3, nctx)),
            pltpu.SemaphoreType.DMA((3,)),
            pltpu.SemaphoreType.REGULAR,
            pltpu.VMEM(lead[:-1] + tails[0], bf16),
            pltpu.VMEM(lead[:-1] + tails[1], bf16),
            pltpu.VMEM(lead + tails[2], bf16),
            pltpu.VMEM((4,) + branch.shape, bf16),
            pltpu.VMEM((4, tq, half), bf16),
            pltpu.VMEM((2, tq, half), bf16),
            pltpu.VMEM((2, 2, unit, round_up(half, 128)), bf16),
            pltpu.VMEM((2, 2, unit, round_up(half, 128)), bf16),
            pltpu.VMEM(tails[1], bf16),
            pltpu.VMEM(tails[1], bf16),
            pltpu.VMEM((nctx, pq, tq), bf16),
            pltpu.VMEM((nctx, pk, tq), bf16),
            pltpu.VMEM((nctx, sr, 128), f32),
            pltpu.VMEM((pq + pk, model), f32),
            pltpu.VMEM((pq + pk, round_up(half, 128)), bf16),
            pltpu.VMEM((pq + pk, round_up(half, 128)), bf16),
            pltpu.VMEM((sr, 128), f32),
            pltpu.VMEM((sr, 128), f32),
            pltpu.SemaphoreType.DMA((2,)),
            pltpu.SemaphoreType.DMA((7,)),
            pltpu.SemaphoreType.DMA((7,)),
            pltpu.SemaphoreType.DMA((2,)),
            pltpu.SemaphoreType.DMA((3, 4, max(nd - 2, 1))),
            pltpu.SemaphoreType.DMA((3, 4, max(nd - 2, 1))),
            pltpu.SemaphoreType.DMA((3, 3)),
            pltpu.SemaphoreType.DMA((3, 3)),
            pltpu.SemaphoreType.DMA((2,)),
            pltpu.SemaphoreType.DMA((2,)),
        ]
        + recvs,
        compiler_params=pltpu.CompilerParams(
            collective_id=1, has_side_effects=True, vmem_limit_bytes=63 * 2**20
        ),
        cost_estimate=pl.CostEstimate(flops=10**10, bytes_accessed=3 * 10**7, transcendentals=10**7),
        name="backward",
    )(docs, q, do, ot, lse, kv, w, cos_t, sin_t, normed, inv, gain, gres, gmlp, low, branch, gup, dnp, inputs)


def rotate(rows, cos_rows, sin_rows):
    half_dim = HS // 2
    first, second = rows[:half_dim], rows[half_dim:]
    return jnp.concatenate(
        [first * cos_rows - second * sin_rows, second * cos_rows + first * sin_rows], axis=0
    )


class Axes:
    def __init__(self, nctx, nf):
        self.ctx, self.f = lax.axis_index("ctx"), lax.axis_index("fsdp")
        self.core, self.place = lax.rem(self.ctx, 2), self.ctx // 2
        self.me = self.ctx * nf + self.f
        self.dims = line_dims(nctx // 2)
        self.nd = len(self.dims)
        ctx, f, core, place = self.ctx, self.f, self.core, self.place
        self.core_axis = (self.nd, 2, core, lambda k: (1 - core, {"ctx": place * 2 + 1 - core, "fsdp": f}))
        self.side_axis = (self.nd + 1, 2, f, lambda k: (1 - f, {"ctx": ctx, "fsdp": 1 - f}))
        self.lines = [self.line(i) for i in range(self.nd)]
        self.peer_count = 2 + sum(size - 1 for size in self.dims)

    def at_line(self, i, there):
        stride = math.prod(self.dims[:i])
        own = lax.rem(self.place // stride, self.dims[i])
        return {"ctx": (self.place + (there - own) * stride) * 2 + self.core, "fsdp": self.f}

    def line(self, i):
        size = self.dims[i]
        own = lax.rem(self.place // math.prod(self.dims[:i]), size)

        def peer(k):
            there = lax.rem(own + k, size)
            return there, self.at_line(i, there)

        return (self.nd - 1 - i, size, own, peer)

    def peers(self):
        found = [self.core_axis[3](1)[1], self.side_axis[3](1)[1]]
        for axis in self.lines:
            found += [axis[3](k)[1] for k in range(1, axis[1])]
        return found

    def place_index(self, j):
        return tuple(
            lax.rem(j // math.prod(self.dims[:i]), self.dims[i]) for i in reversed(range(self.nd))
        )


def forward_kernel(plan, docs, tokens_ref, gains_ref, cos_ref, sin_ref, wq, wk, wv, wo, wg, wu, cot,
                   qt_ref, kv_out, low_ref, ot_ref, lse_ref, wqkv_out, wo_out, gu_out, cots_out,
                   attn_in_ref, inv_ref, gain_ref,
                   wbuf, obuf, gubuf, cbuf, gain_far, own_kv, kvb, m_ref, l_ref, acc_ref,
                   load_sem, w_send, w_recv, top_send, top_recv, ag_send, ag_recv, blk_sem, out_sem):
    nctx, nf, parts, heads, tq = plan
    ax = Axes(nctx, nf)
    f, core, place = ax.f, ax.core, ax.place
    mesh_id = pl.DeviceIdType.MESH
    bf16, f32 = jnp.bfloat16, jnp.float32
    width = tokens_ref.shape[1]
    half = width // nf
    width_q, width_k = 2 * parts * heads * HS, 2 * parts * HS
    rows4, rows2 = half // 4, half // 2
    quarter = gu_out.shape[1] // 2
    side = ax.side_axis[3](1)[1]
    mate = ax.core_axis[3](1)[1]
    low = ax.lines[0]
    bit = lax.rem(low[2], 2)
    across = ax.at_line(0, low[2] + 1 - 2 * bit)
    top = ax.nd - 1
    chunks = ax.dims[top]
    z = ax.lines[top][2]

    barrier = pltpu.get_barrier_semaphore()
    for where in ax.peers():
        pl.semaphore_signal(barrier, inc=1, device_id=where, device_id_type=mesh_id)

    def local(src, dst, i):
        return pltpu.make_async_copy(src, dst, load_sem.at[i])

    own_rows = pl.ds(pl.multiple_of(f * half, half), half)
    own_quarter = pl.ds(pl.multiple_of((2 * f + core) * quarter, quarter), quarter)
    loads = [
        local(wk, wbuf.at[own_rows, pl.ds(width_q, width_k)], 0),
        local(wv, wbuf.at[own_rows, pl.ds(width_q + width_k, width_k)], 1),
        local(wq, wbuf.at[own_rows, pl.ds(0, width_q)], 2),
        local(wo, obuf.at[own_rows], 3),
        local(wg.at[:, own_quarter], gubuf.at[own_rows, pl.ds(0, quarter)], 4),
        local(wu.at[:, own_quarter], gubuf.at[own_rows, pl.ds(quarter, quarter)], 5),
        local(cot, cbuf.at[0], 6),
    ]
    for copy in loads:
        copy.start()

    def remote(src, dst, i, where):
        return pltpu.make_async_remote_copy(
            src_ref=src, dst_ref=dst, send_sem=w_send.at[i], recv_sem=w_recv.at[i],
            device_id=where, device_id_type=mesh_id,
        )

    near = pl.multiple_of(core * rows2 + bit * rows4, 16)
    far_x = pl.multiple_of(core * rows2 + (1 - bit) * rows4, 16)
    there = (1 - f) * half

    def piece(base, offset):
        return pl.ds(pl.multiple_of(base + offset, 16), rows4)

    kv_cols, q_cols = pl.ds(width_q, 2 * width_k), pl.ds(0, width_q)
    mine = f * half
    gains_copy = remote(gains_ref, gain_far, 0, side)
    kv_y = [
        remote(wk.at[piece(0, near)], wbuf.at[piece(mine, near), pl.ds(width_q, width_k)], 1, side),
        remote(wv.at[piece(0, near)], wbuf.at[piece(mine, near), pl.ds(width_q + width_k, width_k)], 2, side),
    ]
    q_y = [remote(wq.at[piece(0, near)], wbuf.at[piece(mine, near), q_cols], 3, side)]
    o_y = [remote(wo.at[piece(0, near)], obuf.at[piece(mine, near)], 4, side)]

    def forwards(buf, cols, first):
        def part(offset):
            return buf.at[piece(there, offset), cols] if cols is not None else buf.at[piece(there, offset)]

        return [
            remote(part(near), part(near), first, across),
            remote(part(near), part(near), first + 1, mate),
            remote(part(far_x), part(far_x), first + 2, mate),
        ]

    kv_f = forwards(wbuf, kv_cols, 5)
    q_f = forwards(wbuf, q_cols, 8)
    o_f = forwards(obuf, None, 11)
    far_quarter = pl.ds(pl.multiple_of((2 * (1 - f) + core) * quarter, quarter), quarter)

    deep = lax.rem(z, 2)
    above = ax.at_line(top, z + 1 - 2 * deep)

    def gu_rows(base, which=bit):
        return pl.ds(pl.multiple_of(base + which * rows2 + deep * rows4, 16), rows4)

    gu_y = [
        remote(wg.at[gu_rows(0), far_quarter], gubuf.at[gu_rows(mine), pl.ds(0, quarter)], 14, side),
        remote(wu.at[gu_rows(0), far_quarter], gubuf.at[gu_rows(mine), pl.ds(quarter, quarter)], 15, side),
    ]
    gu_x = remote(gubuf.at[gu_rows(there)], gubuf.at[gu_rows(there)], 16, across)
    gu_z = [
        remote(gubuf.at[gu_rows(there, which)], gubuf.at[gu_rows(there, which)], 19 + i, above)
        for i, which in enumerate((bit, 1 - bit))
    ]
    cot_y = remote(cot, cbuf.at[1], 17, side)
    cot_c = remote(cbuf.at[pl.ds(0, 2)], cbuf.at[pl.ds(2, 2)], 18, mate)

    pl.semaphore_wait(barrier, ax.peer_count)
    gains_copy.start()
    for copy in kv_y + q_y:
        copy.start()

    hidden = tokens_ref[...].astype(f32)
    inv = lax.rsqrt(jnp.mean(hidden * hidden, axis=1, keepdims=True) + EPS)
    inv_ref[...] = inv
    gains_copy.wait()
    near_gain, far_gain = gains_ref[0:1, :], gain_far[0:1, :]
    gain = jnp.where(
        f == 0,
        jnp.concatenate([near_gain, far_gain], axis=1),
        jnp.concatenate([far_gain, near_gain], axis=1),
    )
    near_mlp, far_mlp = gains_ref[1:2, :], gain_far[1:2, :]
    gain_ref[0:1, :] = gain
    gain_ref[1:2, :] = jnp.where(
        f == 0,
        jnp.concatenate([near_mlp, far_mlp], axis=1),
        jnp.concatenate([far_mlp, near_mlp], axis=1),
    )
    attn_in = (hidden * inv * gain).astype(bf16)
    attn_in_ref[...] = attn_in

    for copy in kv_y:
        copy.wait()
    kv_f[0].start()
    kv_f[1].start()
    for copy in q_y:
        copy.wait()
    for copy in o_y + gu_y:
        copy.start()
    kv_f[0].wait()
    kv_f[2].start()
    q_f[0].start()
    q_f[1].start()
    for copy in loads[:3]:
        copy.wait()
    kv_f[1].wait()
    kv_f[2].wait()
    kv = jnp.dot(attn_in, wbuf[:, width_q:], preferred_element_type=f32)
    cos_rows, sin_rows = cos_ref[...], sin_ref[...]
    kt = jnp.transpose(kv[:, :width_k])
    k_rot = jnp.concatenate(
        [rotate(kt[HS * g : HS * (g + 1)], cos_rows, sin_rows) for g in range(2 * parts)], axis=0
    )
    own_kv[:, :width_k] = jnp.transpose(k_rot).astype(bf16)
    own_kv[:, width_k:] = kv[:, width_k:].astype(bf16)
    own_at = ax.place_index(place) + (core, f)
    put = pltpu.make_async_copy(own_kv, kv_out.at[own_at], out_sem.at[0])
    put.start()

    def top_copy(k):
        return pltpu.make_async_remote_copy(
            src_ref=own_kv, dst_ref=kv_out.at[own_at],
            send_sem=top_send.at[k - 1], recv_sem=top_recv.at[k - 1],
            device_id=ax.at_line(top, lax.rem(z + k, chunks)), device_id_type=mesh_id,
        )

    for k in range(1, chunks):
        @pl.when(z + k < chunks)
        def _():
            top_copy(k).start()

    lower = ax.lines[:top]
    orders = [lower + [ax.side_axis, ax.core_axis], [ax.side_axis] + lower + [ax.core_axis]]
    stages = len(orders[0])

    def ag_copies(k, stage):
        copies = []
        for kind in range(2):
            index = [None] * (ax.nd + 2)
            index[0] = z - k
            for i, axis in enumerate(orders[kind]):
                index[axis[0]] = slice(None) if i < stage else axis[2]
            region = kv_out.at[tuple(index) + (slice(None), pl.ds(kind * width_k, width_k))]
            axis = orders[kind][stage]
            for i in range(1, axis[1]):
                copies.append(
                    pltpu.make_async_remote_copy(
                        src_ref=region, dst_ref=region,
                        send_sem=ag_send.at[k, kind, stage, i - 1],
                        recv_sem=ag_recv.at[k, kind, stage, i - 1],
                        device_id=axis[3](i)[1], device_id_type=mesh_id,
                    )
                )
        return copies

    def tick(k, stage):
        @pl.when(z >= k)
        def _():
            if stage == 0:
                if k > 0:
                    top_copy(k).wait_recv()
            else:
                for copy in ag_copies(k, stage - 1):
                    copy.wait()
            if stage < stages:
                for copy in ag_copies(k, stage):
                    copy.start()

    put.wait()
    tick(0, 0)
    q_f[0].wait()
    q_f[2].start()
    q_f[1].wait()
    q_f[2].wait()
    back = pltpu.make_async_copy(wbuf, wqkv_out, out_sem.at[1])
    back.start()
    query = jnp.dot(attn_in, wbuf[:, :width_q], preferred_element_type=f32)
    query_t = jnp.transpose(query)
    for h in range(2 * parts * heads):
        qt_ref[HS * h : HS * (h + 1), :] = rotate(
            query_t[HS * h : HS * (h + 1)], cos_rows, sin_rows
        ).astype(bf16)
    m_ref[...] = jnp.full_like(m_ref, NEG)
    l_ref[...] = jnp.zeros_like(l_ref)
    acc_ref[...] = jnp.zeros_like(acc_ref)

    bk = 2 * nf * tq
    per_chunk = math.prod(ax.dims[:top])
    start = ax.me * tq

    def block_copy(j, slot):
        return pltpu.make_async_copy(kv_out.at[ax.place_index(j)], kvb.at[slot], blk_sem.at[slot])

    def attend(k):
        first_block = (z - k) * per_chunk
        count = jnp.minimum(place - first_block + 1, per_chunk)

        @pl.when(z >= k)
        def _():
            block_copy(first_block, 0).start()

            def block(i, carry):
                j = first_block + i
                slot = lax.rem(i, 2)

                @pl.when(i + 1 < count)
                def _():
                    block_copy(j + 1, 1 - slot).start()

                block_copy(j, slot).wait()
                bias = bias_tile((start,), docs, j * bk, bk, tq)
                bias = jnp.concatenate([bias] * heads, axis=1)
                for p in range(parts):
                    kb = kvb[slot, :, :, :, 2 * HS * p : 2 * HS * (p + 1)].reshape(bk, 2 * HS)
                    vb = kvb[slot, :, :, :, width_k + 2 * HS * p : width_k + 2 * HS * (p + 1)]
                    vt = jnp.transpose(vb.reshape(bk, 2 * HS))
                    rows = qt_ref[2 * heads * HS * p : 2 * heads * HS * (p + 1), :] * bf16(1.0 / 8.0)
                    for g in range(2):
                        at = 2 * p + g
                        s = jnp.dot(kb, padded(rows, heads, g), preferred_element_type=f32) + bias
                        m = m_ref[at]
                        new = jnp.maximum(m, jnp.max(s, axis=0, keepdims=True))
                        prob = jnp.exp(s - new)
                        decay = jnp.exp(m - new)
                        m_ref[at] = new
                        l_ref[at] = l_ref[at] * decay + jnp.sum(prob, axis=0, keepdims=True)
                        acc_ref[at] = acc_ref[at] * decay + jnp.dot(
                            vt[HS * g : HS * (g + 1)], prob.astype(bf16), preferred_element_type=f32
                        )
                return carry

            lax.fori_loop(0, count, block, 0)

    for turn in range(1, chunks + stages):
        for k in range(chunks):
            stage = turn - k
            if (k, stage) != (0, 0) and 0 <= stage <= stages:
                tick(k, stage)
        if turn == 4:
            for copy in o_y + gu_y:
                copy.wait()
            o_f[0].start()
            o_f[1].start()
            gu_x.start()
            gu_z[0].start()
        if turn == 3:
            cot_y.start()
        if turn == 6:
            o_f[0].wait()
            o_f[2].start()
            gu_x.wait()
            gu_z[1].start()
        if turn == 5:
            cot_y.wait()
            loads[6].wait()
            cot_c.start()
        if turn >= stages:
            attend(turn - stages)
    for p in range(parts):
        outs = []
        for g in range(2):
            at = 2 * p + g
            out = acc_ref[at] / l_ref[at]
            outs.append(out)
            ot_ref[at] = out
            lse_ref[at] = m_ref[at] + jnp.log(l_ref[at])
        low_ref[:, 2 * heads * HS * p : 2 * heads * HS * (p + 1)] = head_lanes(outs, heads, tq).astype(bf16)

    for k in range(1, chunks):
        @pl.when(z + k < chunks)
        def _():
            top_copy(k).wait_send()
    for copy in loads[3:6]:
        copy.wait()
    backs = [back]
    for waits, src, dst in (
        (o_f[1:], obuf, wo_out), ([cot_c], cbuf, cots_out), (gu_z, gubuf, gu_out)
    ):
        for copy in waits:
            copy.wait()
        backs.append(pltpu.make_async_copy(src, dst, out_sem.at[1 + len(backs)]))
        backs[-1].start()
    for copy in backs:
        copy.wait()


def forward(nctx, nf, docs, tokens, gains, cos_t, sin_t, wq, wk, wv, wo, wg, wu, cot):
    tq, width = tokens.shape
    width_q, width_k = wq.shape[1], wk.shape[1]
    parts = width_k // (2 * HS)
    heads = width_q // HS // (2 * parts)
    hidden_units = wg.shape[1]
    quarter = hidden_units // (2 * nf)
    dims = line_dims(nctx // 2)
    lead = tuple(reversed(dims))
    most = max(dims + [2])
    chunks = dims[-1]
    stages = len(dims) + 1
    bf16, f32 = jnp.bfloat16, jnp.float32
    vmem = pl.BlockSpec(memory_space=pltpu.VMEM)
    smem = pl.BlockSpec(memory_space=pltpu.SMEM)
    hbm = pl.BlockSpec(memory_space=pl.ANY)
    dma = pltpu.SemaphoreType.DMA
    return pl.pallas_call(
        functools.partial(forward_kernel, (nctx, nf, parts, heads, tq)),
        out_shape=[
            jax.ShapeDtypeStruct((width_q, tq), bf16),
            jax.ShapeDtypeStruct(lead + (2, nf, tq, 2 * width_k), bf16),
            jax.ShapeDtypeStruct((tq, width_q), bf16),
            jax.ShapeDtypeStruct((2 * parts, HS, heads * tq), f32),
            jax.ShapeDtypeStruct((2 * parts, 1, heads * tq), f32),
            jax.ShapeDtypeStruct((width, width_q + 2 * width_k), bf16),
            jax.ShapeDtypeStruct((nf * wo.shape[0], wo.shape[1]), bf16),
            jax.ShapeDtypeStruct((width, 2 * quarter), bf16),
            jax.ShapeDtypeStruct((2 * nf, tq, width), bf16),
            jax.ShapeDtypeStruct((tq, width), bf16),
            jax.ShapeDtypeStruct((tq, 1), f32),
            jax.ShapeDtypeStruct((2, width), f32),
        ],
        in_specs=[smem, vmem, vmem, vmem, vmem] + [hbm] * 7,
        out_specs=[vmem, hbm, vmem, vmem, vmem, hbm, hbm, hbm, hbm, vmem, vmem, vmem],
        scratch_shapes=[
            pltpu.VMEM((width, width_q + 2 * width_k), bf16),
            pltpu.VMEM((nf * wo.shape[0], wo.shape[1]), bf16),
            pltpu.VMEM((width, 2 * quarter), bf16),
            pltpu.VMEM((2 * nf, tq, width), bf16),
            pltpu.VMEM(gains.shape, f32),
            pltpu.VMEM((tq, 2 * width_k), bf16),
            pltpu.VMEM((2, 2, nf, tq, 2 * width_k), bf16),
            pltpu.VMEM((2 * parts, 1, heads * tq), f32),
            pltpu.VMEM((2 * parts, 1, heads * tq), f32),
            pltpu.VMEM((2 * parts, HS, heads * tq), f32),
            dma((7,)),
            dma((21,)),
            dma((21,)),
            dma((chunks - 1,)),
            dma((chunks - 1,)),
            dma((chunks, 2, stages, most - 1)),
            dma((chunks, 2, stages, most - 1)),
            dma((2,)),
            dma((5,)),
        ],
        compiler_params=pltpu.CompilerParams(
            collective_id=0, has_side_effects=True, vmem_limit_bytes=60 * 2**20
        ),
        name="forward",
    )(docs, tokens, gains, cos_t, sin_t, wq, wk, wv, wo, wg, wu, cot)


def feed_forward_kernel(plan, tokens_ref, low_ref, attn_in_ref, gains_ref, wo_hbm, gu_hbm, down_hbm, cots_hbm,
                        result_ref, gres_ref, branch_ref, gattn_ref, gmlp_ref, gup_ref, dnp_ref, inputs_out,
                        wo, gu, down, cots, xs, grads, mixed, gm, sums, sent, core_in, side_in, side_out,
                        load_sem, x_send, x_recv, s_send, s_recv, top_send, top_recv,
                        ag_send, ag_recv, out_sem):
    nctx, nf = plan
    ax = Axes(nctx, nf)
    f, core, place = ax.f, ax.core, ax.place
    mesh_id = pl.DeviceIdType.MESH
    bf16, f32 = jnp.bfloat16, jnp.float32
    tq, width = tokens_ref.shape
    quarter = down.shape[0]
    side = ax.side_axis[3](1)[1]
    mate = ax.core_axis[3](1)[1]
    top = ax.nd - 1
    chunks = ax.dims[top]
    z = ax.lines[top][2]

    barrier = pltpu.get_barrier_semaphore()
    for where in ax.peers():
        pl.semaphore_signal(barrier, inc=1, device_id=where, device_id_type=mesh_id)
    loads = [
        pltpu.make_async_copy(src, dst, load_sem.at[i])
        for i, (src, dst) in enumerate((
            (wo_hbm, wo), (cots_hbm, cots),
            (down_hbm.at[pl.ds(pl.multiple_of(core * quarter, quarter), quarter)], down), (gu_hbm, gu),
        ))
    ]
    for copy in loads:
        copy.start()

    def remote(src, dst, sends, recvs, i, where):
        return pltpu.make_async_remote_copy(
            src_ref=src, dst_ref=dst, send_sem=sends.at[i], recv_sem=recvs.at[i],
            device_id=where, device_id_type=mesh_id,
        )

    hidden = tokens_ref[...].astype(f32)
    own_at = ax.place_index(place) + (core,)
    put = pltpu.make_async_copy(attn_in_ref, inputs_out.at[own_at], out_sem.at[0])

    def top_copy(k):
        return pltpu.make_async_remote_copy(
            src_ref=attn_in_ref, dst_ref=inputs_out.at[own_at],
            send_sem=top_send.at[k - 1], recv_sem=top_recv.at[k - 1],
            device_id=ax.at_line(top, lax.rem(z + k, chunks)), device_id_type=mesh_id,
        )

    order = ax.lines[:top] + [ax.core_axis]
    stages = len(order)

    def ag_copies(k, stage):
        index = [None] * (ax.nd + 1)
        index[0] = lax.rem(z + chunks - k, chunks)
        for i, axis in enumerate(order):
            index[axis[0]] = slice(None) if i < stage else axis[2]
        region = inputs_out.at[tuple(index)]
        axis = order[stage]
        return [
            pltpu.make_async_remote_copy(
                src_ref=region, dst_ref=region,
                send_sem=ag_send.at[k, stage, i - 1], recv_sem=ag_recv.at[k, stage, i - 1],
                device_id=axis[3](i)[1], device_id_type=mesh_id,
            )
            for i in range(1, axis[1])
        ]

    def tick(turn):
        for k in range(chunks):
            stage = turn - k
            if not 0 <= stage <= stages:
                continue
            if stage == 0:
                if k > 0:
                    top_copy(k).wait()
                else:
                    put.wait()
            else:
                for copy in ag_copies(k, stage - 1):
                    copy.wait()
            if stage < stages:
                for copy in ag_copies(k, stage):
                    copy.start()

    pl.semaphore_wait(barrier, ax.peer_count)
    put.start()
    for k in range(1, chunks):
        top_copy(k).start()
    tick(0)

    loads[0].wait()
    resid = hidden + jnp.dot(low_ref[...], wo[...], preferred_element_type=f32)
    inv = lax.rsqrt(jnp.mean(resid * resid, axis=1, keepdims=True) + EPS)
    normed = resid * inv
    gain = gains_ref[1:2, :]
    xs[0] = (normed * gain).astype(bf16)
    x_side = remote(xs.at[0], xs.at[1], x_send, x_recv, 0, side)
    x_core = remote(xs.at[0], xs.at[2], x_send, x_recv, 1, mate)
    x_far = remote(xs.at[1], xs.at[3], x_send, x_recv, 2, mate)
    x_side.start()
    x_core.start()

    def rows(slot):
        return slice(slot * tq, (slot + 1) * tq)

    for copy in loads[1:3]:
        copy.wait()
    gm[...] = lax.dot_general(
        cots[...].reshape(4 * tq, width), down[...], (((1,), (1,)), ((), ())), preferred_element_type=f32
    )
    loads[3].wait()
    step = 256

    def both(ref, a, b, span=slice(None)):
        return jnp.concatenate([ref[a, :, span], ref[b, :, span]], axis=0)

    def compute(a, b):
        x = both(xs, a, b)
        for n in range(quarter // step):
            span = slice(n * step, (n + 1) * step)
            up_span = slice(quarter + n * step, quarter + (n + 1) * step)
            gate = jnp.dot(x, gu[:, span], preferred_element_type=f32)
            up = jnp.dot(x, gu[:, up_span], preferred_element_type=f32)
            sig = jax.nn.sigmoid(gate)
            act = gate * sig
            grad = jnp.concatenate([gm[rows(a), span], gm[rows(b), span]], axis=0)
            mix = (act * up).astype(bf16)
            grad_gate = (grad * up * sig * (1.0 + gate * (1.0 - sig))).astype(bf16)
            grad_up = (grad * act).astype(bf16)
            for i, slot in enumerate((a, b)):
                mixed[slot, :, span] = mix[rows(i)]
                grads[slot, :, span] = grad_gate[rows(i)]
                grads[slot, :, up_span] = grad_up[rows(i)]
        total = lax.dot_general(
            both(grads, a, b), gu[...], (((1,), (1,)), ((), ())), preferred_element_type=f32
        )
        for i, slot in enumerate((a, b)):
            sums[0, slot] = total[rows(i)]

    def outputs(a, b):
        total = jnp.dot(both(mixed, a, b), down[...], preferred_element_type=f32)
        for i, slot in enumerate((a, b)):
            sums[1, slot] = total[rows(i)]

    def to_core(kind, slot):
        i = 2 * kind + slot - 2
        return remote(sent.at[i], core_in.at[i], s_send, s_recv, i, mate)

    def to_side(kind):
        return remote(side_out.at[kind], side_in.at[kind], s_send, s_recv, 4 + kind, side)

    def give_core(kind, slot):
        sent[2 * kind + slot - 2] = sums[kind, slot].astype(bf16)
        to_core(kind, slot).start()

    def give_side(kind):
        to_core(kind, 3).wait()
        side_out[kind] = (sums[kind, 1] + core_in[2 * kind + 1].astype(f32)).astype(bf16)
        to_side(kind).start()

    x_core.wait()
    compute(0, 2)
    give_core(0, 2)
    x_side.wait()
    x_far.start()
    outputs(0, 2)
    give_core(1, 2)
    x_far.wait()
    compute(1, 3)
    give_core(0, 3)
    tick(1)
    outputs(1, 3)
    give_side(0)
    give_core(1, 3)
    flat_x = xs[...].reshape(4 * tq, width)
    pieces = nctx // 2
    unit = quarter // pieces
    tall = max(unit, 256)
    for kind in range(2):
        for n in range(quarter // tall):
            span = slice(kind * quarter + n * tall, kind * quarter + (n + 1) * tall)
            cols = jnp.transpose(jnp.concatenate([grads[s, :, span] for s in range(4)], axis=0))
            part = jnp.dot(cols, flat_x, preferred_element_type=f32).astype(bf16)
            first = n * tall
            while first < (n + 1) * tall:
                piece, at = first // unit, first % unit
                end = min((piece + 1) * unit, (n + 1) * tall)
                gup_ref[static_index(bit_dims(nctx // 2), piece) + (kind, slice(at, at + end - first))] = part[
                    first - n * tall : end - n * tall
                ]
                first = end
        if kind == 0:
            give_side(1)
            tick(2)
    unit = width // pieces
    flat_mixed = mixed[...].reshape(4 * tq, quarter)
    for n in range(width // 384):
        cols = jnp.transpose(jnp.concatenate([cots[s, :, 384 * n : 384 * (n + 1)] for s in range(4)], axis=0))
        part = jnp.dot(cols, flat_mixed, preferred_element_type=f32).astype(bf16)
        first = n * 384
        while first < (n + 1) * 384:
            piece, at = first // unit, first % unit
            end = min((piece + 1) * unit, (n + 1) * 384)
            rows_of = part[first - n * 384 : end - n * 384]
            for c in range(quarter // 128):
                dnp_ref[
                    static_index(bit_dims(nctx // 2), piece)
                    + (slice(c * unit + at, c * unit + at + end - first),)
                ] = rows_of[:, 128 * c : 128 * (c + 1)]
            first = end

    to_core(0, 2).wait()
    to_side(0).wait()
    grad = sums[0, 0] + core_in[0].astype(f32) + side_in[0].astype(f32)
    product = grad * normed
    gmlp_ref[...] = jnp.sum(product, axis=0, keepdims=True)
    scaled = grad * gain
    mean = jnp.mean(scaled * normed, axis=1, keepdims=True)
    gres = cots[0].astype(f32) + inv * (scaled - normed * mean)
    gres_ref[...] = gres
    branch = gres.astype(bf16)
    branch_ref[...] = branch
    gattn_ref[...] = lax.dot_general(
        branch, wo[...], (((1,), (1,)), ((), ())), preferred_element_type=f32
    ).astype(bf16)
    tick(3)
    to_core(1, 2).wait()
    to_side(1).wait()
    result_ref[...] = (resid + sums[1, 0] + core_in[2].astype(f32) + side_in[1].astype(f32)).astype(bf16)
    for turn in range(4, chunks + stages):
        tick(turn)


def static_index(dims, piece):
    return tuple(piece // math.prod(dims[:i]) % dims[i] for i in reversed(range(len(dims))))


def feed_forward(nctx, nf, tokens, low, attn_in, gains, wo, gu, down, cots):
    tq, width = tokens.shape
    quarter = gu.shape[1] // 2
    dims = line_dims(nctx // 2)
    bits = bit_dims(nctx // 2)
    lead = tuple(reversed(dims))
    plane = nctx // 2
    chunks, stages, most = dims[-1], len(dims), max(dims + [2])
    bf16, f32 = jnp.bfloat16, jnp.float32
    vmem = pl.BlockSpec(memory_space=pltpu.VMEM)
    hbm = pl.BlockSpec(memory_space=pl.ANY)
    dma = pltpu.SemaphoreType.DMA
    return pl.pallas_call(
        functools.partial(feed_forward_kernel, (nctx, nf)),
        out_shape=[
            jax.ShapeDtypeStruct((tq, width), bf16),
            jax.ShapeDtypeStruct((tq, width), f32),
            jax.ShapeDtypeStruct((tq, width), bf16),
            jax.ShapeDtypeStruct((tq, width), bf16),
            jax.ShapeDtypeStruct((1, width), f32),
            jax.ShapeDtypeStruct(tuple(bits) + (2, quarter // plane, width), bf16),
            jax.ShapeDtypeStruct(tuple(bits) + (width // plane * (quarter // 128), 128), bf16),
            jax.ShapeDtypeStruct(lead + (2, tq, width), bf16),
        ],
        in_specs=[vmem] * 4 + [hbm] * 4,
        out_specs=[vmem] * 7 + [hbm],
        scratch_shapes=[
            pltpu.VMEM(wo.shape, bf16),
            pltpu.VMEM(gu.shape, bf16),
            pltpu.VMEM((quarter, width), bf16),
            pltpu.VMEM((4, tq, width), bf16),
            pltpu.VMEM((4, tq, width), bf16),
            pltpu.VMEM((4, tq, 2 * quarter), bf16),
            pltpu.VMEM((4, tq, quarter), bf16),
            pltpu.VMEM((4 * tq, quarter), f32),
            pltpu.VMEM((2, 4, tq, width), f32),
            pltpu.VMEM((4, tq, width), bf16),
            pltpu.VMEM((4, tq, width), bf16),
            pltpu.VMEM((2, tq, width), bf16),
            pltpu.VMEM((2, tq, width), bf16),
            dma((4,)),
            dma((4,)),
            dma((4,)),
            dma((6,)),
            dma((6,)),
            dma((chunks - 1,)),
            dma((chunks - 1,)),
            dma((chunks, stages, most - 1)),
            dma((chunks, stages, most - 1)),
            dma((1,)),
        ],
        compiler_params=pltpu.CompilerParams(
            collective_id=2, has_side_effects=True, vmem_limit_bytes=60 * 2**20
        ),
        name="feed_forward",
    )(tokens, low, attn_in, gains, wo, gu, down, cots)


def per_device(
    nctx,
    nf,
    tokens,
    query_weight,
    key_projection,
    value_projection,
    output_weight,
    gate_weight,
    up_weight,
    down_weight,
    norm_attn,
    norm_mlp,
    doc_starts,
    cotangent,
):
    token_rows, width = tokens.shape
    n_tokens = token_rows * nctx * nf
    bf16, f32 = jnp.bfloat16, jnp.float32

    own_device = lax.axis_index(AXES)
    own_index = layout_rows(own_device, token_rows)
    own_begin = doc_begin(own_index, doc_starts)
    cosine_table, sine_table = rope_tables(own_index - own_begin)
    cosine_table, sine_table = cosine_table.T, sine_table.T
    gains = jnp.pad(jnp.stack([norm_attn, norm_mlp]).astype(f32), ((0, 6), (0, 0)))
    (
        query_rot, key_values, attn_low, attn_exact, log_total, qkv_full, output_full, gate_up,
        cotangents, attention_input, inv_attn, gains,
    ) = forward(
        nctx, nf, doc_starts, tokens, gains, cosine_table, sine_table, query_weight, key_projection,
        value_projection, output_weight, gate_weight, up_weight, cotangent,
    )
    key_width = KEY_VALUE_HEADS * HEAD_SIZE
    key_values = key_values.reshape(n_tokens, 2 * key_width)
    result, grad_resid, grad_branch, grad_attn, gain_mlp_partial, gate_up_partial, down_partial, inputs_all = feed_forward(
        nctx, nf, tokens, attn_low, attention_input, gains, output_full, gate_up, down_weight,
        cotangents.reshape(2 * nf, token_rows, width),
    )

    tokens_grad, query_sum, key_sum, value_sum, gain_sums, gate_sum, up_sum, down_sum, output_sum = backward(
        nctx, nf, doc_starts, query_rot, grad_attn, attn_exact, log_total, key_values, qkv_full,
        cosine_table, sine_table, tokens, inv_attn, gains, grad_resid,
        gain_mlp_partial, attn_low, grad_branch, gate_up_partial, down_partial,
        inputs_all.reshape(nctx, token_rows, width),
    )

    gain_sums = gain_sums[: 2 * width // 128].reshape(2, width)
    return (
        result,
        tokens_grad,
        query_sum.T,
        key_sum.T,
        value_sum.T,
        output_sum.T,
        gate_sum.T,
        up_sum.T,
        down_sum.T,
        gain_sums[0],
        gain_sums[1],
    )


def solution(mesh):
    return jax.shard_map(
        functools.partial(per_device, mesh.shape["ctx"], mesh.shape["fsdp"]),
        mesh=mesh,
        in_specs=(
            P(("ctx", "fsdp"), None),
            P("fsdp", None),
            P("fsdp", None),
            P("fsdp", None),
            P("fsdp", None),
            P("fsdp", None),
            P("fsdp", None),
            P("fsdp", None),
            P("fsdp"),
            P("fsdp"),
            P(),
            P(("ctx", "fsdp"), None),
        ),
        out_specs=(
            P(("ctx", "fsdp"), None),
            P(("ctx", "fsdp"), None),
            P("fsdp", "ctx"),
            P("fsdp", "ctx"),
            P("fsdp", "ctx"),
            P("fsdp", "ctx"),
            P("fsdp", "ctx"),
            P("fsdp", "ctx"),
            P("fsdp", "ctx"),
            P(),
            P(),
        ),
        check_vma=False,
    )
```

profile of v0, /device:TPU:15, one launch (start us, length us, event | category | flops | bytes accessed | tf_op | source)
XLA Modules:
  0.0 312.1 jit_solution(1574652224983190577)
XLA Ops:
  0.7 0.7 select_reduce_fusion
  1.4 0.7 stack.9
  2.1 0.7 stack.10
  2.8 0.6 fusion.3.gains_ref
  3.4 0.8 multiply_sine_fusion
  4.2 84.0 %forward.1 = (bf16[1152,128]{1,0:T(8,128)(2,1)}, bf16[4,2,2,2,128,768]{5,4,3,2,1,0:T(8,128)(2,1)}, bf16[128,1152]{1,0:T(8,128)(2,1)}, f32[6,64,384]{2,1,0:T(8,12...) custom-call(s32[4]{0:T(128)} %docs.3, ...), custom_call_target="tpu_custom_call" | custom-call | tf_op jit(solution)/shard_map/forward/pallas_call | solution.py:1226
  88.1 54.0 %feed_forward.1 = (bf16[128,1152]{1,0:T(8,128)(2,1)}, f32[128,1152]{1,0:T(8,128)}, bf16[128,1152]{1,0:T(8,128)(2,1)}, bf16[128,1152]{1,0:T(8,128)(2,1)}, f32[1,1...) custom-call(bf16[128,1152]{1,0:T(8,128)(2,1)} %normed_ref.1, ...), custom_call_target="tpu_custom_call" | custom-call | tf_op jit(solution)/shard_map/feed_forward/pallas_call | solution.py:1521
  142.1 0.0 copy-start.2
  142.1 156.4 %backward.1 = (f32[128,1152]{1,0:T(8,128)}, f32[72,576]{1,0:T(8,128)}, f32[24,576]{1,0:T(8,128)}, f32[24,576]{1,0:T(8,128)}, f32[24,128]{1,0:T(8,128)}, /*index=...) custom-call(s32[4]{0:T(128)} %docs.3, bf16[1152,128]{1,0:T(8,128)(2,1)} %get-tuple-element.47.q_ref, ...), custom_call_target="tpu_custom_call" | custom-call | flops 10000000000 | bytes 30000000 | tf_op jit(solution)/shard_map/backward/pallas_call | solution.py:771
  298.5 0.0 copy-start
  298.5 0.0 copy-start.1
  298.5 1.4 slice_bitcast_fusion
  299.9 0.0 copy-done.2
  299.9 0.7 copy.32
  300.6 1.9 copy.33
  302.6 1.6 copy.34
  304.2 1.5 copy.35
  305.6 1.5 copy.36
  307.1 1.6 copy.37
  308.7 1.8 copy.38
  310.5 0.0 copy-done
  310.5 0.8 copy.39
  311.3 0.0 copy-done.1
  311.3 0.8 copy.40
  (3 shorter events, 0.0 us)
Async XLA Ops:
  142.1 157.8 %copy-start.2 = (bf16[128,1152]{1,0:T(8,128)(2,1)S(1)}, bf16[128,1152]{1,0:T(8,128)(2,1)}, u32[]{:S(2)}) copy-start(bf16[128,1152]{1,0:T(8,128)(2,1)} %get-tuple-element.84) | copy-start | bytes 884740
  298.5 12.0 %copy-start = (f32[192,576]{1,0:T(8,128)S(1)}, f32[192,576]{1,0:T(8,128)}, u32[]{:S(2)}) copy-start(f32[192,576]{1,0:T(8,128)} %get-tuple-element.66) | copy-start | bytes 1327108
  298.5 12.8 %copy-start.1 = (f32[72,1536]{1,0:T(8,128)S(1)}, f32[72,1536]{1,0:T(8,128)}, u32[]{:S(2)}) copy-start(f32[72,1536]{1,0:T(8,128)} %get-tuple-element.67) | copy-start | bytes 1327108
where the time goes:
time: 314 us; the launch traced here: 312 us
  Pallas kernels  294 us (94%)
  local copies, waits for them, and re-layouts  14.9 us (5%)
    pallas_call x1, Pallas kernels, backward(): pl.pallas_call(functools.partial(backward_kernel, (nctx, nf, parts, heads...  156 us
    pallas_call x1, Pallas kernels, forward(): pl.pallas_call(functools.partial(forward_kernel, (nctx, nf, parts, heads,...  84 us
    pallas_call x1, Pallas kernels, feed_forward(): pl.pallas_call(functools.partial(feed_forward_kernel, (nctx, nf)), out_sh...  54 us
    unnamed x15, local copies, waits for them, and re-layouts  12.1 us

commit v1 on v0

--- a/solution.py
+++ b/solution.py
@@ -183,14 +183,14 @@
     core_axis = (nd, 2, core, lambda k: (1 - core, {"ctx": place * 2 + 1 - core, "fsdp": me_f}))
     side_axis = (nd + 1, 2, me_f, lambda k: (1 - me_f, {"ctx": me_c, "fsdp": 1 - me_f}))
     lines = [dim_axis(i) for i in range(nd)]
-    orders = [[core_axis, side_axis] + lines, [core_axis, lines[0], side_axis] + lines[1:]]
+    orders = [[core_axis, side_axis] + lines, [core_axis, side_axis] + w_order(lines)]
     stages = nd + 2
     wrecvs = recvs[2 * stages :]
     side_at, mate_at = side_axis[3](1)[1], core_axis[3](1)[1]
 
     low_bits = nd - 2
-    arrays = ((wg, gup_hbm), (wd, dnp_hbm), (wo, None))
-    w_lines = [lines, w_order(lines), lines]
+    arrays = ((wg, gup_hbm, (0,)), (wd, dnp_hbm, ()), (wo, None, ()), (wg, gup_hbm, (1,)))
+    w_lines = [lines, w_order(lines), w_order(lines), lines]
 
     def chunk_at(a, k):
         near, far_line = w_lines[a][nd - 2], w_lines[a][nd - 1]
@@ -209,14 +209,14 @@
 
     def held(a, index):
         first = w_lines[a][0][0]
-        return index if a == 2 else index[:first] + index[first + 1 :]
+        return index if a == 2 else index[:first] + index[first + 1 :] + arrays[a][2]
 
     def w_copy(a, k, stage):
-        buf, far = arrays[a]
+        buf, far, sub = arrays[a]
         there, where = w_lines[a][stage][3](1)
         index = w_region(a, k, stage, there)
         return pltpu.make_async_remote_copy(
-            src_ref=far.at[index] if stage == 0 and a < 2 else buf.at[held(a, index)],
+            src_ref=far.at[index + sub] if stage == 0 and a != 2 else buf.at[held(a, index)],
             dst_ref=wrecvs[a * (low_bits + 2) + stage].at[chunk_at(a, k)],
             send_sem=w_send.at[a, k, stage], recv_sem=w_recv.at[a, k, stage],
             device_id=where, device_id_type=mesh_id,
@@ -272,7 +272,7 @@
 
     w_loads = [
         pltpu.make_async_copy(far.at[(slice(None),) * w_lines[i][0][0] + (w_lines[i][0][2],)], buf, w_load.at[i])
-        for i, (buf, far) in enumerate(arrays[:2])
+        for i, (buf, far, _) in enumerate(arrays[:2])
     ]
     for copy in w_loads:
         copy.start()
@@ -315,8 +315,8 @@
     pl.semaphore_wait(barrier, n - 1)
     low_side.start()
     br_side.start()
-    w_start((0, 1), 0)
-    w_start((0, 1), 1)
+    for k in range(4):
+        w_start((0, 3, 1) if k < 2 else (1,), k)
 
     def region(kind, stage, at):
         index = [slice(None)] * (nd + 2)
@@ -503,13 +503,12 @@
         if p == 1:
             for copy in w_loads:
                 copy.wait()
-            w_finish((0, 1), 0)
-            w_start((0, 1), 2)
-            output_partial()
-            for k in range(4):
-                w_start((2,), k)
-    w_finish((0, 1), 1)
-    w_start((0, 1), 3)
+            for k in range(2):
+                w_finish((0, 3), k)
+                w_start((0, 3), k + 2)
+    for k in range(2):
+        w_finish((1,), k)
+    output_partial()
 
     def copies_to(k, which):
         other = lax.rem(me_c + k, nctx)
@@ -548,8 +547,8 @@
         qblk[i, 0:cq, :] = gqt_ref[cq * i : cq * (i + 1), :]
     share(0)
     ga_ref[...] = jnp.dot(w_ref[:, :width_q], gqt_ref[...], preferred_element_type=jnp.float32)
-    for k in range(2):
-        w_finish((2,), k)
+    for k in range(4):
+        w_start((2,), k)
     pq, pk = qblk.shape[1], kvblk.shape[1]
 
     def columns(col_ref, first, count):
@@ -576,16 +575,49 @@
 
         lax.fori_loop(0, nctx, one, 0)
 
+    per_side = plane // 2
+    home = (2 * me_f + core) * per_side + place // 2
+    slot = lax.rem(place, 2)
+
+    def home_copy(kind, s):
+        return pltpu.make_async_remote_copy(
+            src_ref=fin.at[kind, s], dst_ref=fin_in.at[kind, slot],
+            send_sem=fin_send.at[kind, s], recv_sem=fin_recv.at[kind, slot],
+            device_id={"ctx": home, "fsdp": jnp.int32(s)}, device_id_type=mesh_id,
+        )
+
+    def self_copy(kind, s):
+        return pltpu.make_async_copy(fin.at[kind, s], fin_in.at[kind, slot], fin_send.at[kind, s])
+
+    def to_homes(kind, a):
+        total = w_total(a)
+        unit, lanes = fin.shape[2], fin.shape[3]
+        blank = jnp.zeros((unit, lanes - half), fin.dtype)
+        for s in range(2):
+            fin[kind, s] = jnp.concatenate([total[:, half * s : half * (s + 1)].astype(fin.dtype), blank], axis=1)
+            at_home = (home == me_c) & (me_f == s)
+
+            @pl.when(jnp.logical_not(at_home))
+            def _():
+                home_copy(kind, s).start()
+
+            @pl.when(at_home)
+            def _():
+                self_copy(kind, s).start()
+
     turn = 0
     while progress:
         for p in list(progress):
             advance(p)
         if turn == 0:
-            w_finish((0, 1, 2), 2)
+            for k in range(2, 4):
+                w_finish((0, 3, 1), k)
         if turn == 1:
-            w_finish((0, 1, 2), 3)
-            share_wait(0)
-            columns(colq_ref, 0, pq)
+            for k in range(2):
+                w_finish((2,), k)
+        if turn == 2:
+            for k in range(2, 4):
+                w_finish((2,), k)
         turn += 1
 
     cos_rows, sin_rows = cos_ref[...], sin_ref[...]
@@ -623,39 +655,14 @@
     mean = jnp.mean(scaled * normed, axis=1, keepdims=True)
     tokens_ref[...] = gres_ref[...] + inv_ref[...] * (scaled - normed * mean)
 
-    total = w_total(0)
-    unit, lanes = fin.shape[2], fin.shape[3]
-    blank = jnp.zeros((2, unit, lanes - half), fin.dtype)
-    for s in range(2):
-        fin[s] = jnp.concatenate([total[:, :, half * s : half * (s + 1)].astype(fin.dtype), blank], axis=2)
+    to_homes(0, 0)
+    share_wait(0)
+    columns(colq_ref, 0, pq)
+    to_homes(1, 3)
     dsum = w_total(1)
     dsend[...] = dsum.astype(dsend.dtype)
     down_copy = g_copy(4, dsend, din, mate_at)
     down_copy.start()
-    per_side = plane // 2
-    home = (2 * me_f + core) * per_side + place // 2
-    slot = lax.rem(place, 2)
-
-    def home_copy(s):
-        return pltpu.make_async_remote_copy(
-            src_ref=fin.at[s], dst_ref=fin_in.at[slot], send_sem=fin_send.at[s], recv_sem=fin_recv.at[slot],
-            device_id={"ctx": home, "fsdp": jnp.int32(s)}, device_id_type=mesh_id,
-        )
-
-    def self_copy(s):
-        return pltpu.make_async_copy(fin.at[s], fin_in.at[slot], fin_send.at[s])
-
-    for s in range(2):
-        at_home = (home == me_c) & (me_f == s)
-
-        @pl.when(jnp.logical_not(at_home))
-        def _():
-            home_copy(s).start()
-
-        @pl.when(at_home)
-        def _():
-            self_copy(s).start()
-
     osum = w_total(2)
     out_ref[...] = osum[: out_ref.shape[0], :half]
     share_wait(1)
@@ -696,30 +703,32 @@
         jnp.concatenate([own_cols, far_cols], axis=1),
         jnp.concatenate([far_cols, own_cols], axis=1),
     )
-    for s in range(2):
-        at_home = (home == me_c) & (me_f == s)
-
-        @pl.when(jnp.logical_not(at_home))
-        def _():
-            home_copy(s).wait_send()
-
-        @pl.when(at_home)
-        def _():
-            self_copy(s).wait()
-
     owner = me_c // per_side
-    for h in range(2):
-        holder = (2 * lax.rem(me_c, per_side) + h) * 2 + lax.rem(owner, 2)
-
-        @pl.when(jnp.logical_not((holder == me_c) & (owner // 2 == me_f)))
-        def _():
-            pltpu.make_async_remote_copy(
-                src_ref=fin.at[0], dst_ref=fin_in.at[h], send_sem=fin_send.at[0], recv_sem=fin_recv.at[h],
-                device_id={"ctx": home, "fsdp": me_f}, device_id_type=mesh_id,
-            ).wait_recv()
+    for kind in range(2):
+        for s in range(2):
+            at_home = (home == me_c) & (me_f == s)
+
+            @pl.when(jnp.logical_not(at_home))
+            def _():
+                home_copy(kind, s).wait_send()
+
+            @pl.when(at_home)
+            def _():
+                self_copy(kind, s).wait()
+
+        for h in range(2):
+            holder = (2 * lax.rem(me_c, per_side) + h) * 2 + lax.rem(owner, 2)
+
+            @pl.when(jnp.logical_not((holder == me_c) & (owner // 2 == me_f)))
+            def _():
+                pltpu.make_async_remote_copy(
+                    src_ref=fin.at[0, 0], dst_ref=fin_in.at[kind, h],
+                    send_sem=fin_send.at[0, 0], recv_sem=fin_recv.at[kind, h],
+                    device_id={"ctx": home, "fsdp": me_f}, device_id_type=mesh_id,
+                ).wait_recv()
 
     for kind, ref in ((0, gate_ref), (1, up_ref)):
-        rows = jnp.concatenate([fin_in[0, kind], fin_in[1, kind]], axis=0).astype(jnp.float32)
+        rows = jnp.concatenate([fin_in[kind, 0], fin_in[kind, 1]], axis=0).astype(jnp.float32)
         ref[...] = rows[:, :half]
 
 
@@ -739,7 +748,7 @@
     line = [(nd - 1 - i, dims[i]) for i in range(nd)]
     orders = [
         [axes["core"], axes["side"]] + line,
-        [axes["core"], line[0], axes["side"]] + line[1:],
+        [axes["core"], axes["side"]] + w_order(line),
     ]
     recvs = []
     for order in orders:
@@ -755,7 +764,7 @@
     quarter = dnp.shape[-2] // deep * 128
     plane = nctx // 2
     tails = [gup.shape[nd:], dnp.shape[nd:], (round_up(deep // 2, 16), round_up(half, 128))]
-    for tail in tails:
+    for tail in (tails[0][1:], tails[1], tails[2], tails[0][1:]):
         for stage in range(nd - 2):
             recvs.append(pltpu.VMEM((2,) * (nd - 1 - stage) + tail, bf16))
         recvs += [pltpu.VMEM((2,) + tail, bf16), pltpu.VMEM((1,) + tail, bf16)]
@@ -821,12 +830,12 @@
             pltpu.SemaphoreType.DMA((7,)),
             pltpu.SemaphoreType.DMA((7,)),
             pltpu.SemaphoreType.DMA((2,)),
-            pltpu.SemaphoreType.DMA((3, 4, max(nd - 2, 1))),
-            pltpu.SemaphoreType.DMA((3, 4, max(nd - 2, 1))),
-            pltpu.SemaphoreType.DMA((3, 3)),
-            pltpu.SemaphoreType.DMA((3, 3)),
-            pltpu.SemaphoreType.DMA((2,)),
-            pltpu.SemaphoreType.DMA((2,)),
+            pltpu.SemaphoreType.DMA((4, 4, max(nd - 2, 1))),
+            pltpu.SemaphoreType.DMA((4, 4, max(nd - 2, 1))),
+            pltpu.SemaphoreType.DMA((4, 3)),
+            pltpu.SemaphoreType.DMA((4, 3)),
+            pltpu.SemaphoreType.DMA((2, 2)),
+            pltpu.SemaphoreType.DMA((2, 2)),
         ]
         + recvs,
         compiler_params=pltpu.CompilerParams(
@@ -1564,6 +1573,38 @@
     )(tokens, low, attn_in, gains, wo, gu, down, cots)
 
 
+def finish_kernel(result, tokens, q, k, v, o, gate, up, down, gains, *outs):
+    outs[0][...] = result[...]
+    outs[1][...] = tokens[...]
+    for src, dst in zip((q, k, v, o, gate, up, down), outs[2:9]):
+        dst[...] = jnp.transpose(src[...])
+    tiles = outs[9].shape[1] // 128
+    for i in range(2):
+        outs[9 + i][...] = jnp.concatenate(
+            [gains[tiles * i + j : tiles * i + j + 1, :] for j in range(tiles)], axis=1
+        )
+
+
+def finish(nf, width, result, tokens, *sums):
+    weights, gains = sums[:-1], sums[-1]
+    f32 = jnp.float32
+    vmem = pl.BlockSpec(memory_space=pltpu.VMEM)
+    outs = pl.pallas_call(
+        finish_kernel,
+        out_shape=[
+            jax.ShapeDtypeStruct(result.shape, result.dtype),
+            jax.ShapeDtypeStruct(tokens.shape, f32),
+        ]
+        + [jax.ShapeDtypeStruct(w.shape[::-1], f32) for w in weights]
+        + [jax.ShapeDtypeStruct((1, width), f32)] * 2,
+        in_specs=[vmem] * 10,
+        out_specs=[vmem] * 11,
+        compiler_params=pltpu.CompilerParams(vmem_limit_bytes=32 * 2**20),
+        name="finish",
+    )(result, tokens, *weights, gains)
+    return tuple(outs[:9]) + (outs[9].reshape(width), outs[10].reshape(width))
+
+
 def per_device(
     nctx,
     nf,
@@ -1611,19 +1652,9 @@
         inputs_all.reshape(nctx, token_rows, width),
     )
 
-    gain_sums = gain_sums[: 2 * width // 128].reshape(2, width)
-    return (
-        result,
-        tokens_grad,
-        query_sum.T,
-        key_sum.T,
-        value_sum.T,
-        output_sum.T,
-        gate_sum.T,
-        up_sum.T,
-        down_sum.T,
-        gain_sums[0],
-        gain_sums[1],
+    return finish(
+        nf, width, result, tokens_grad, query_sum, key_sum, value_sum, output_sum, gate_sum, up_sum,
+        down_sum, gain_sums,
     )
 
 

time: 314 us -> 298 us (0.949)
  Pallas kernels: 294 us -> 275 us
    pallas_call x1, Pallas kernels: 156 us -> 135 us  [backward(): pl.pallas_call(functools.partial(backward_kernel, (nctx, nf, parts, heads...]
    unnamed x15 -> x27, local copies, waits for them, and re-layouts: 12.1 us -> 14.5 us
where the time goes in v1:
time: 298 us; the launch traced here: 295 us
  Pallas kernels  275 us (92%)
  local copies, waits for them, and re-layouts  15.9 us (5%)
  other arithmetic  3.37 us (1%)
    pallas_call x1, Pallas kernels, backward(): pl.pallas_call(functools.partial(backward_kernel, (nctx, nf, parts, heads...  135 us
    pallas_call x1, Pallas kernels, forward(): pl.pallas_call(functools.partial(forward_kernel, (nctx, nf, parts, heads,...  84 us
    pallas_call x1, Pallas kernels, feed_forward(): pl.pallas_call(functools.partial(feed_forward_kernel, (nctx, nf)), out_sh...  54 us
    unnamed x27, local copies, waits for them, and re-layouts  14.5 us

profile of v1, /device:TPU:15, one launch (start us, length us, event | category | flops | bytes accessed | tf_op | source)
XLA Modules:
  0.0 294.7 jit_solution(16797117412772259404)
XLA Ops:
  0.7 0.7 select_reduce_fusion
  1.4 0.7 stack.9
  2.1 0.7 stack.10
  2.8 0.6 fusion.3.gains_ref
  3.4 0.8 multiply_sine_fusion
  4.2 84.0 %forward.1 = (bf16[1152,128]{1,0:T(8,128)(2,1)}, bf16[4,2,2,2,128,768]{5,4,3,2,1,0:T(8,128)(2,1)}, bf16[128,1152]{1,0:T(8,128)(2,1)}, f32[6,64,384]{2,1,0:T(8,12...) custom-call(s32[4]{0:T(128)} %docs.3, ...), custom_call_target="tpu_custom_call" | custom-call | tf_op jit(solution)/shard_map/forward/pallas_call | solution.py:1235
  88.1 54.0 %feed_forward.1 = (bf16[128,1152]{1,0:T(8,128)(2,1)}, f32[128,1152]{1,0:T(8,128)}, bf16[128,1152]{1,0:T(8,128)(2,1)}, bf16[128,1152]{1,0:T(8,128)(2,1)}, f32[1,1...) custom-call(bf16[128,1152]{1,0:T(8,128)(2,1)} %normed_ref.1, ...), custom_call_target="tpu_custom_call" | custom-call | tf_op jit(solution)/shard_map/feed_forward/pallas_call | solution.py:1530
  142.2 0.0 copy-start.4
  142.2 135.0 %backward.1 = (f32[128,1152]{1,0:T(8,128)}, f32[72,576]{1,0:T(8,128)}, f32[24,576]{1,0:T(8,128)}, f32[24,576]{1,0:T(8,128)}, f32[24,128]{1,0:T(8,128)}, /*index=...) custom-call(s32[4]{0:T(128)} %docs.3, bf16[1152,128]{1,0:T(8,128)(2,1)} %get-tuple-element.58.q_ref, ...), custom_call_target="tpu_custom_call" | custom-call | flops 10000000000 | bytes 30000000 | tf_op jit(solution)/shard_map/backward/pallas_call | solution.py:780
  277.2 0.0 copy-done.4
  277.2 0.0 copy-start
  277.2 1.1 copy-done
  278.3 0.0 copy-start.1
  278.3 1.0 copy-done.1
  279.3 0.0 copy-start.2
  279.3 1.0 copy-done.2
  280.3 0.0 copy-start.3
  280.3 1.0 copy-done.3
  281.3 0.0 copy-start.5
  281.4 0.9 copy-done.5
  282.3 0.0 copy-start.6
  282.3 0.9 copy-done.6
  283.2 0.0 copy-start.7
  283.2 0.8 copy-done.7
  284.0 0.0 copy-start.8
  284.0 0.8 copy-done.8
  284.9 0.0 copy-start.9
  284.9 0.7 copy-done.9
  285.6 1.8 finish.1
  287.3 0.6 reduce
  287.9 0.6 reduce.1
  288.6 0.8 copy.31
  289.3 0.8 copy.32
  290.1 0.8 copy.30
  290.9 0.8 copy.33
  291.7 1.0 copy.36
  292.7 1.0 copy.34
  293.7 1.0 copy.35
  (3 shorter events, 0.0 us)
Async XLA Ops:
  142.2 135.0 %copy-start.4 = (bf16[128,1152]{1,0:T(8,128)(2,1)S(1)}, bf16[128,1152]{1,0:T(8,128)(2,1)}, u32[]{:S(2)}) copy-start(bf16[128,1152]{1,0:T(8,128)(2,1)} %get-tuple-element.57.result) | copy-start | bytes 884740
  277.2 1.1 copy-start
  278.3 1.0 copy-start.1
  279.3 1.0 copy-start.2
  280.3 1.0 copy-start.3
  281.3 0.9 copy-start.5
  282.3 0.9 copy-start.6
  283.2 0.8 copy-start.7
  284.0 0.8 copy-start.8
  284.9 0.7 copy-start.9

commit v2 on v1

--- a/solution.py
+++ b/solution.py
@@ -1364,8 +1364,7 @@
 
     pl.semaphore_wait(barrier, ax.peer_count)
     put.start()
-    for k in range(1, chunks):
-        top_copy(k).start()
+    top_copy(1).start()
     tick(0)
 
     loads[0].wait()
@@ -1389,6 +1388,7 @@
         cots[...].reshape(4 * tq, width), down[...], (((1,), (1,)), ((), ())), preferred_element_type=f32
     )
     loads[3].wait()
+    top_copy(2).start()
     step = 256
 
     def both(ref, a, b, span=slice(None)):
@@ -1441,14 +1441,16 @@
     x_core.wait()
     compute(0, 2)
     give_core(0, 2)
+    top_copy(3).start()
     x_side.wait()
     x_far.start()
+    tick(1)
     outputs(0, 2)
     give_core(1, 2)
     x_far.wait()
     compute(1, 3)
     give_core(0, 3)
-    tick(1)
+    tick(2)
     outputs(1, 3)
     give_side(0)
     give_core(1, 3)
@@ -1471,7 +1473,7 @@
                 first = end
         if kind == 0:
             give_side(1)
-            tick(2)
+            tick(3)
     unit = width // pieces
     flat_mixed = mixed[...].reshape(4 * tq, quarter)
     for n in range(width // 384):
@@ -1489,6 +1491,7 @@
                 ] = rows_of[:, 128 * c : 128 * (c + 1)]
             first = end
 
+    tick(4)
     to_core(0, 2).wait()
     to_side(0).wait()
     grad = sums[0, 0] + core_in[0].astype(f32) + side_in[0].astype(f32)
@@ -1503,11 +1506,10 @@
     gattn_ref[...] = lax.dot_general(
         branch, wo[...], (((1,), (1,)), ((), ())), preferred_element_type=f32
     ).astype(bf16)
-    tick(3)
     to_core(1, 2).wait()
     to_side(1).wait()
     result_ref[...] = (resid + sums[1, 0] + core_in[2].astype(f32) + side_in[1].astype(f32)).astype(bf16)
-    for turn in range(4, chunks + stages):
+    for turn in range(5, chunks + stages):
         tick(turn)
 
 
@@ -1585,21 +1587,25 @@
         )
 
 
-def finish(nf, width, result, tokens, *sums):
+def finish(width, result, tokens, *sums):
     weights, gains = sums[:-1], sums[-1]
     f32 = jnp.float32
-    vmem = pl.BlockSpec(memory_space=pltpu.VMEM)
+
+    def whole(x):
+        return pl.BlockSpec(x.shape, lambda i: (0,) * len(x.shape))
+
+    shapes = (
+        [jax.ShapeDtypeStruct(result.shape, result.dtype), jax.ShapeDtypeStruct(tokens.shape, f32)]
+        + [jax.ShapeDtypeStruct(w.shape[::-1], f32) for w in weights]
+        + [jax.ShapeDtypeStruct((1, width), f32)] * 2
+    )
     outs = pl.pallas_call(
         finish_kernel,
-        out_shape=[
-            jax.ShapeDtypeStruct(result.shape, result.dtype),
-            jax.ShapeDtypeStruct(tokens.shape, f32),
-        ]
-        + [jax.ShapeDtypeStruct(w.shape[::-1], f32) for w in weights]
-        + [jax.ShapeDtypeStruct((1, width), f32)] * 2,
-        in_specs=[vmem] * 10,
-        out_specs=[vmem] * 11,
-        compiler_params=pltpu.CompilerParams(vmem_limit_bytes=32 * 2**20),
+        grid=(1,),
+        out_shape=shapes,
+        in_specs=[whole(x) for x in (result, tokens) + sums],
+        out_specs=[whole(x) for x in shapes],
+        compiler_params=pltpu.CompilerParams(vmem_limit_bytes=60 * 2**20),
         name="finish",
     )(result, tokens, *weights, gains)
     return tuple(outs[:9]) + (outs[9].reshape(width), outs[10].reshape(width))
@@ -1653,7 +1659,7 @@
     )
 
     return finish(
-        nf, width, result, tokens_grad, query_sum, key_sum, value_sum, output_sum, gate_sum, up_sum,
+        width, result, tokens_grad, query_sum, key_sum, value_sum, output_sum, gate_sum, up_sum,
         down_sum, gain_sums,
     )
 

time: 298 us -> 301 us (1.010)
    unnamed x27 -> x9, local copies, waits for them, and re-layouts: 14.5 us -> 12.2 us
where the time goes in v2:
time: 301 us; the launch traced here: 297 us
  Pallas kernels  278 us (92%)
  local copies, waits for them, and re-layouts  13.6 us (5%)
  other arithmetic  4.81 us (2%)
    pallas_call x1, Pallas kernels, backward(): pl.pallas_call(functools.partial(backward_kernel, (nctx, nf, parts, heads...  136 us
    pallas_call x1, Pallas kernels, forward(): pl.pallas_call(functools.partial(forward_kernel, (nctx, nf, parts, heads,...  84 us
    pallas_call x1, Pallas kernels, feed_forward(): pl.pallas_call(functools.partial(feed_forward_kernel, (nctx, nf)), out_sh...  54.1 us
    unnamed x9, local copies, waits for them, and re-layouts  12.2 us

profile of v2, /device:TPU:15, one launch (start us, length us, event | category | flops | bytes accessed | tf_op | source)
XLA Modules:
  0.0 297.5 jit_solution(16674946038165328566)
XLA Ops:
  0.7 0.7 select_reduce_fusion
  1.4 0.7 stack.9
  2.1 0.7 stack.10
  2.8 0.6 fusion.3.gains_ref
  3.4 0.8 multiply_sine_fusion
  4.2 84.0 %forward.1 = (bf16[1152,128]{1,0:T(8,128)(2,1)}, bf16[4,2,2,2,128,768]{5,4,3,2,1,0:T(8,128)(2,1)}, bf16[128,1152]{1,0:T(8,128)(2,1)}, f32[6,64,384]{2,1,0:T(8,12...) custom-call(s32[4]{0:T(128)} %docs.3, ...), custom_call_target="tpu_custom_call" | custom-call | tf_op jit(solution)/shard_map/forward/pallas_call | solution.py:1235
  88.1 54.1 %feed_forward.1 = (bf16[128,1152]{1,0:T(8,128)(2,1)}, f32[128,1152]{1,0:T(8,128)}, bf16[128,1152]{1,0:T(8,128)(2,1)}, bf16[128,1152]{1,0:T(8,128)(2,1)}, f32[1,1...) custom-call(bf16[128,1152]{1,0:T(8,128)(2,1)} %normed_ref.1, ...), custom_call_target="tpu_custom_call" | custom-call | tf_op jit(solution)/shard_map/feed_forward/pallas_call | solution.py:1532
  142.3 136.2 %backward.1 = (f32[128,1152]{1,0:T(8,128)}, f32[72,576]{1,0:T(8,128)}, f32[24,576]{1,0:T(8,128)}, f32[24,576]{1,0:T(8,128)}, f32[24,128]{1,0:T(8,128)}, /*index=...) custom-call(s32[4]{0:T(128)} %docs.3, bf16[1152,128]{1,0:T(8,128)(2,1)} %get-tuple-element.58.q_ref, ...), custom_call_target="tpu_custom_call" | custom-call | flops 10000000000 | bytes 30000000 | tf_op jit(solution)/shard_map/backward/pallas_call | solution.py:780
  278.5 4.1 %finish.1 = (bf16[128,1152]{1,0:T(8,128)(2,1)}, f32[128,1152]{1,0:T(8,128)}, f32[576,72]{1,0:T(8,128)}, f32[576,24]{1,0:T(8,128)}, f32[576,24]{1,0:T(8,128)}, /*...) custom-call(bf16[128,1152]{1,0:T(8,128)(2,1)} %get-tuple-element.57., ...), custom_call_target="tpu_custom_call" | custom-call | tf_op jit(solution)/shard_map/finish/pallas_call | solution.py:1602
  282.6 0.0 copy-start
  282.6 1.4 reduce
  284.0 1.3 reduce.1
  285.3 1.7 copy.31
  287.0 1.7 copy.32
  288.7 1.8 copy.30
  290.5 1.8 copy.33
  292.3 2.1 copy.36
  294.4 2.1 copy.34
  296.5 0.0 copy-done
  296.5 1.0 copy.35
  (3 shorter events, 0.0 us)
Async XLA Ops:
  282.6 13.9 %copy-start = (f32[576,192]{1,0:T(8,128)S(1)}, f32[576,192]{1,0:T(8,128)}, u32[]{:S(2)}) copy-start(f32[576,192]{1,0:T(8,128)} %get-tuple-element.109) | copy-start | bytes 1327108

commit v3 on v2

--- a/solution.py
+++ b/solution.py
@@ -1575,40 +1575,25 @@
     )(tokens, low, attn_in, gains, wo, gu, down, cots)
 
 
-def finish_kernel(result, tokens, q, k, v, o, gate, up, down, gains, *outs):
-    outs[0][...] = result[...]
-    outs[1][...] = tokens[...]
-    for src, dst in zip((q, k, v, o, gate, up, down), outs[2:9]):
-        dst[...] = jnp.transpose(src[...])
-    tiles = outs[9].shape[1] // 128
-    for i in range(2):
-        outs[9 + i][...] = jnp.concatenate(
-            [gains[tiles * i + j : tiles * i + j + 1, :] for j in range(tiles)], axis=1
-        )
-
-
-def finish(width, result, tokens, *sums):
-    weights, gains = sums[:-1], sums[-1]
-    f32 = jnp.float32
-
+def finish_kernel(*refs):
+    count = len(refs) // 2
+    for src, dst in zip(refs[:count], refs[count:]):
+        dst[...] = src[...]
+
+
+def finish(*values):
     def whole(x):
         return pl.BlockSpec(x.shape, lambda i: (0,) * len(x.shape))
 
-    shapes = (
-        [jax.ShapeDtypeStruct(result.shape, result.dtype), jax.ShapeDtypeStruct(tokens.shape, f32)]
-        + [jax.ShapeDtypeStruct(w.shape[::-1], f32) for w in weights]
-        + [jax.ShapeDtypeStruct((1, width), f32)] * 2
-    )
-    outs = pl.pallas_call(
+    return pl.pallas_call(
         finish_kernel,
         grid=(1,),
-        out_shape=shapes,
-        in_specs=[whole(x) for x in (result, tokens) + sums],
-        out_specs=[whole(x) for x in shapes],
+        out_shape=[jax.ShapeDtypeStruct(x.shape, x.dtype) for x in values],
+        in_specs=[whole(x) for x in values],
+        out_specs=[whole(x) for x in values],
         compiler_params=pltpu.CompilerParams(vmem_limit_bytes=60 * 2**20),
         name="finish",
-    )(result, tokens, *weights, gains)
-    return tuple(outs[:9]) + (outs[9].reshape(width), outs[10].reshape(width))
+    )(*values)
 
 
 def per_device(
@@ -1658,10 +1643,11 @@
         inputs_all.reshape(nctx, token_rows, width),
     )
 
-    return finish(
-        width, result, tokens_grad, query_sum, key_sum, value_sum, output_sum, gate_sum, up_sum,
-        down_sum, gain_sums,
+    gain_sums = gain_sums[: 2 * width // 128].reshape(2, width)
+    result, tokens_grad, *sums = finish(
+        result, tokens_grad, query_sum, key_sum, value_sum, output_sum, gate_sum, up_sum, down_sum
     )
+    return (result, tokens_grad, *(weight.T for weight in sums), gain_sums[0], gain_sums[1])
 
 
 def solution(mesh):

time: 301 us -> 287 us (0.953)
  local copies, waits for them, and re-layouts: 13.6 us -> 2.75 us
    unnamed x9 -> x0, local copies, waits for them, and re-layouts: 12.2 us -> none
where the time goes in v3:
time: 287 us; the launch traced here: 283 us
  Pallas kernels  277 us (97%)
    pallas_call x1, Pallas kernels, backward(): pl.pallas_call(functools.partial(backward_kernel, (nctx, nf, parts, heads...  136 us
    pallas_call x1, Pallas kernels, forward(): pl.pallas_call(functools.partial(forward_kernel, (nctx, nf, parts, heads,...  84 us
    pallas_call x1, Pallas kernels, feed_forward(): pl.pallas_call(functools.partial(feed_forward_kernel, (nctx, nf)), out_sh...  54.1 us

profile of v3, /device:TPU:15, one launch (start us, length us, event | category | flops | bytes accessed | tf_op | source)
XLA Modules:
  0.0 283.0 jit_solution(14600500517435339593)
XLA Ops:
  0.7 0.7 select_reduce_fusion
  1.4 0.7 stack.9
  2.1 0.7 stack.10
  2.8 0.6 fusion.3.gains_ref
  3.4 0.8 multiply_sine_fusion
  4.2 84.0 %forward.1 = (bf16[1152,128]{1,0:T(8,128)(2,1)}, bf16[4,2,2,2,128,768]{5,4,3,2,1,0:T(8,128)(2,1)}, bf16[128,1152]{1,0:T(8,128)(2,1)}, f32[6,64,384]{2,1,0:T(8,12...) custom-call(s32[4]{0:T(128)} %docs.3, ...), custom_call_target="tpu_custom_call" | custom-call | tf_op jit(solution)/shard_map/forward/pallas_call | solution.py:1235
  88.1 54.1 %feed_forward.1 = (bf16[128,1152]{1,0:T(8,128)(2,1)}, f32[128,1152]{1,0:T(8,128)}, bf16[128,1152]{1,0:T(8,128)(2,1)}, bf16[128,1152]{1,0:T(8,128)(2,1)}, f32[1,1...) custom-call(bf16[128,1152]{1,0:T(8,128)(2,1)} %normed_ref.1, ...), custom_call_target="tpu_custom_call" | custom-call | tf_op jit(solution)/shard_map/feed_forward/pallas_call | solution.py:1532
  142.3 136.0 %backward.1 = (f32[128,1152]{1,0:T(8,128)}, f32[72,576]{1,0:T(8,128)}, f32[24,576]{1,0:T(8,128)}, f32[24,576]{1,0:T(8,128)}, f32[24,128]{1,0:T(8,128)}, /*index=...) custom-call(s32[4]{0:T(128)} %docs.3, bf16[1152,128]{1,0:T(8,128)(2,1)} %get-tuple-element.56.q_ref, ...), custom_call_target="tpu_custom_call" | custom-call | flops 10000000000 | bytes 30000000 | tf_op jit(solution)/shard_map/backward/pallas_call | solution.py:780
  278.3 3.4 %finish.1 = (bf16[128,1152]{1,0:T(8,128)(2,1)}, f32[128,1152]{1,0:T(8,128)}, f32[72,576]{1,0:T(8,128)}, f32[24,576]{1,0:T(8,128)}, f32[24,576]{1,0:T(8,128)}, /*...) custom-call(bf16[128,1152]{1,0:T(8,128)(2,1)} %get-tuple-element.55.refs_0_, ...), custom_call_target="tpu_custom_call" | custom-call | tf_op jit(solution)/shard_map/finish/pallas_call | solution.py:1588
  281.6 1.4 slice_bitcast_fusion
  (3 shorter events, 0.0 us)

commit v4 on v3

--- a/solution.py
+++ b/solution.py
@@ -658,6 +658,18 @@
     to_homes(0, 0)
     share_wait(0)
     columns(colq_ref, 0, pq)
+
+    def give_half(first, count, i):
+        rows = slice(first, first + count)
+        theirs = jnp.where(me_f == 0, cols_acc[rows, half:], cols_acc[rows, :half]).astype(half_send.dtype)
+        side_pad = jnp.zeros((count, half_send.shape[1] - half), half_send.dtype)
+        half_send[rows, :] = jnp.concatenate([theirs, side_pad], axis=1)
+        span = pl.ds(first, count)
+        copy = g_copy(i, half_send.at[span], half_in.at[span], side_at)
+        copy.start()
+        return copy
+
+    half_q = give_half(0, pq, 5)
     to_homes(1, 3)
     dsum = w_total(1)
     dsend[...] = dsum.astype(dsend.dtype)
@@ -667,11 +679,7 @@
     out_ref[...] = osum[: out_ref.shape[0], :half]
     share_wait(1)
     columns(colkv_ref, pq, pk)
-    left, right = cols_acc[:, :half], cols_acc[:, half:]
-    side_pad = jnp.zeros((pq + pk, half_send.shape[1] - half), half_send.dtype)
-    half_send[...] = jnp.concatenate([jnp.where(me_f == 0, right, left).astype(half_send.dtype), side_pad], axis=1)
-    half_copy = g_copy(5, half_send, half_in, side_at)
-    half_copy.start()
+    half_kv = give_half(pq, pk, 7)
     share_wait(2)
     gain_total = gains_ref[0]
     for i in range(1, nctx):
@@ -679,7 +687,8 @@
     gain_send[...] = gain_total
     gain_copy = g_copy(6, gain_send, gain_in, side_at)
     gain_copy.start()
-    half_copy.wait()
+    half_q.wait()
+    half_kv.wait()
     own_half = jnp.where(me_f == 0, cols_acc[:, :half], cols_acc[:, half:])
     rows = own_half + half_in[:, :half].astype(jnp.float32)
     query_ref[...] = rows[:cq]
@@ -827,8 +836,8 @@
             pltpu.VMEM((sr, 128), f32),
             pltpu.VMEM((sr, 128), f32),
             pltpu.SemaphoreType.DMA((2,)),
-            pltpu.SemaphoreType.DMA((7,)),
-            pltpu.SemaphoreType.DMA((7,)),
+            pltpu.SemaphoreType.DMA((8,)),
+            pltpu.SemaphoreType.DMA((8,)),
             pltpu.SemaphoreType.DMA((2,)),
             pltpu.SemaphoreType.DMA((4, 4, max(nd - 2, 1))),
             pltpu.SemaphoreType.DMA((4, 4, max(nd - 2, 1))),

time: 287 us -> 285 us (level)
  no operation moved by 1% of the time
where the time goes in v4:
time: 285 us; the launch traced here: 282 us
  Pallas kernels  276 us (97%)
    pallas_call x1, Pallas kernels, backward(): pl.pallas_call(functools.partial(backward_kernel, (nctx, nf, parts, heads...  135 us
    pallas_call x1, Pallas kernels, forward(): pl.pallas_call(functools.partial(forward_kernel, (nctx, nf, parts, heads,...  84 us
    pallas_call x1, Pallas kernels, feed_forward(): pl.pallas_call(functools.partial(feed_forward_kernel, (nctx, nf)), out_sh...  54.1 us

profile of v4, /device:TPU:15, one launch (start us, length us, event | category | flops | bytes accessed | tf_op | source)
XLA Modules:
  0.0 281.7 jit_solution(3637074945691730075)
XLA Ops:
  0.7 0.7 select_reduce_fusion
  1.4 0.7 stack.9
  2.1 0.7 stack.10
  2.8 0.6 fusion.3.gains_ref
  3.4 0.8 multiply_sine_fusion
  4.2 84.0 %forward.1 = (bf16[1152,128]{1,0:T(8,128)(2,1)}, bf16[4,2,2,2,128,768]{5,4,3,2,1,0:T(8,128)(2,1)}, bf16[128,1152]{1,0:T(8,128)(2,1)}, f32[6,64,384]{2,1,0:T(8,12...) custom-call(s32[4]{0:T(128)} %docs.3, ...), custom_call_target="tpu_custom_call" | custom-call | tf_op jit(solution)/shard_map/forward/pallas_call | solution.py:1244
  88.1 54.1 %feed_forward.1 = (bf16[128,1152]{1,0:T(8,128)(2,1)}, f32[128,1152]{1,0:T(8,128)}, bf16[128,1152]{1,0:T(8,128)(2,1)}, bf16[128,1152]{1,0:T(8,128)(2,1)}, f32[1,1...) custom-call(bf16[128,1152]{1,0:T(8,128)(2,1)} %normed_ref.1, ...), custom_call_target="tpu_custom_call" | custom-call | tf_op jit(solution)/shard_map/feed_forward/pallas_call | solution.py:1541
  142.3 134.6 %backward.1 = (f32[128,1152]{1,0:T(8,128)}, f32[72,576]{1,0:T(8,128)}, f32[24,576]{1,0:T(8,128)}, f32[24,576]{1,0:T(8,128)}, f32[24,128]{1,0:T(8,128)}, /*index=...) custom-call(s32[4]{0:T(128)} %docs.3, bf16[1152,128]{1,0:T(8,128)(2,1)} %get-tuple-element.56.q_ref, ...), custom_call_target="tpu_custom_call" | custom-call | flops 10000000000 | bytes 30000000 | tf_op jit(solution)/shard_map/backward/pallas_call | solution.py:789
  276.9 3.4 %finish.1 = (bf16[128,1152]{1,0:T(8,128)(2,1)}, f32[128,1152]{1,0:T(8,128)}, f32[72,576]{1,0:T(8,128)}, f32[24,576]{1,0:T(8,128)}, f32[24,576]{1,0:T(8,128)}, /*...) custom-call(bf16[128,1152]{1,0:T(8,128)(2,1)} %get-tuple-element.55.refs_0_, ...), custom_call_target="tpu_custom_call" | custom-call | tf_op jit(solution)/shard_map/finish/pallas_call | solution.py:1597
  280.3 1.4 slice_bitcast_fusion
  (3 shorter events, 0.0 us)

commit v5 on v4

--- a/solution.py
+++ b/solution.py
@@ -903,10 +903,10 @@
         )
 
 
-def forward_kernel(plan, docs, tokens_ref, gains_ref, cos_ref, sin_ref, wq, wk, wv, wo, wg, wu, cot,
+def forward_kernel(plan, docs, tokens_ref, norm_attn_ref, norm_mlp_ref, cos_ref, sin_ref, wq, wk, wv, wo, wg, wu, cot,
                    qt_ref, kv_out, low_ref, ot_ref, lse_ref, wqkv_out, wo_out, gu_out, cots_out,
                    attn_in_ref, inv_ref, gain_ref,
-                   wbuf, obuf, gubuf, cbuf, gain_far, own_kv, kvb, m_ref, l_ref, acc_ref,
+                   wbuf, obuf, gubuf, cbuf, gains_ref, gain_far, own_kv, kvb, m_ref, l_ref, acc_ref,
                    load_sem, w_send, w_recv, top_send, top_recv, ag_send, ag_recv, blk_sem, out_sem):
     nctx, nf, parts, heads, tq = plan
     ax = Axes(nctx, nf)
@@ -1004,6 +1004,9 @@
     cot_y = remote(cot, cbuf.at[1], 17, side)
     cot_c = remote(cbuf.at[pl.ds(0, 2)], cbuf.at[pl.ds(2, 2)], 18, mate)
 
+    gains_ref[...] = jnp.zeros_like(gains_ref)
+    gains_ref[0:1, :] = norm_attn_ref[...].astype(f32)
+    gains_ref[1:2, :] = norm_mlp_ref[...].astype(f32)
     pl.semaphore_wait(barrier, ax.peer_count)
     gains_copy.start()
     for copy in kv_y + q_y:
@@ -1224,7 +1227,7 @@
         copy.wait()
 
 
-def forward(nctx, nf, docs, tokens, gains, cos_t, sin_t, wq, wk, wv, wo, wg, wu, cot):
+def forward(nctx, nf, docs, tokens, norm_attn, norm_mlp, cos_t, sin_t, wq, wk, wv, wo, wg, wu, cot):
     tq, width = tokens.shape
     width_q, width_k = wq.shape[1], wk.shape[1]
     parts = width_k // (2 * HS)
@@ -1257,14 +1260,15 @@
             jax.ShapeDtypeStruct((tq, 1), f32),
             jax.ShapeDtypeStruct((2, width), f32),
         ],
-        in_specs=[smem, vmem, vmem, vmem, vmem] + [hbm] * 7,
+        in_specs=[smem, vmem, vmem, vmem, vmem, vmem] + [hbm] * 7,
         out_specs=[vmem, hbm, vmem, vmem, vmem, hbm, hbm, hbm, hbm, vmem, vmem, vmem],
         scratch_shapes=[
             pltpu.VMEM((width, width_q + 2 * width_k), bf16),
             pltpu.VMEM((nf * wo.shape[0], wo.shape[1]), bf16),
             pltpu.VMEM((width, 2 * quarter), bf16),
             pltpu.VMEM((2 * nf, tq, width), bf16),
-            pltpu.VMEM(gains.shape, f32),
+            pltpu.VMEM((8, norm_attn.shape[1]), f32),
+            pltpu.VMEM((8, norm_attn.shape[1]), f32),
             pltpu.VMEM((tq, 2 * width_k), bf16),
             pltpu.VMEM((2, 2, nf, tq, 2 * width_k), bf16),
             pltpu.VMEM((2 * parts, 1, heads * tq), f32),
@@ -1284,7 +1288,7 @@
             collective_id=0, has_side_effects=True, vmem_limit_bytes=60 * 2**20
         ),
         name="forward",
-    )(docs, tokens, gains, cos_t, sin_t, wq, wk, wv, wo, wg, wu, cot)
+    )(docs, tokens, norm_attn, norm_mlp, cos_t, sin_t, wq, wk, wv, wo, wg, wu, cot)
 
 
 def feed_forward_kernel(plan, tokens_ref, low_ref, attn_in_ref, gains_ref, wo_hbm, gu_hbm, down_hbm, cots_hbm,
@@ -1630,12 +1634,11 @@
     own_begin = doc_begin(own_index, doc_starts)
     cosine_table, sine_table = rope_tables(own_index - own_begin)
     cosine_table, sine_table = cosine_table.T, sine_table.T
-    gains = jnp.pad(jnp.stack([norm_attn, norm_mlp]).astype(f32), ((0, 6), (0, 0)))
     (
         query_rot, key_values, attn_low, attn_exact, log_total, qkv_full, output_full, gate_up,
         cotangents, attention_input, inv_attn, gains,
     ) = forward(
-        nctx, nf, doc_starts, tokens, gains, cosine_table, sine_table, query_weight, key_projection,
+        nctx, nf, doc_starts, tokens, norm_attn[None], norm_mlp[None], cosine_table, sine_table, query_weight, key_projection,
         value_projection, output_weight, gate_weight, up_weight, cotangent,
     )
     key_width = KEY_VALUE_HEADS * HEAD_SIZE

time: 285 us -> 286 us (level)
  no operation moved by 1% of the time
where the time goes in v5:
time: 286 us; the launch traced here: 282 us
  Pallas kernels  276 us (97%)
  local copies, waits for them, and re-layouts  3.9 us (1%)
    pallas_call x1, Pallas kernels, backward(): pl.pallas_call(functools.partial(backward_kernel, (nctx, nf, parts, heads...  135 us
    pallas_call x1, Pallas kernels, forward(): pl.pallas_call(functools.partial(forward_kernel, (nctx, nf, parts, heads,...  84 us
    pallas_call x1, Pallas kernels, feed_forward(): pl.pallas_call(functools.partial(feed_forward_kernel, (nctx, nf)), out_sh...  54.1 us

profile of v5, /device:TPU:15, one launch (start us, length us, event | category | flops | bytes accessed | tf_op | source)
XLA Modules:
  0.0 282.2 jit_solution(17564686986331544929)
XLA Ops:
  0.7 0.7 select_reduce_fusion
  1.4 1.3 broadcast_in_dim.14.norm_attn_ref
  2.7 1.3 broadcast_in_dim.22.norm_mlp_ref
  4.0 0.8 multiply_sine_fusion
  4.7 84.0 %forward.1 = (bf16[1152,128]{1,0:T(8,128)(2,1)}, bf16[4,2,2,2,128,768]{5,4,3,2,1,0:T(8,128)(2,1)}, bf16[128,1152]{1,0:T(8,128)(2,1)}, f32[6,64,384]{2,1,0:T(8,12...) custom-call(s32[4]{0:T(128)} %docs.3, ...), custom_call_target="tpu_custom_call" | custom-call | tf_op jit(solution)/shard_map/forward/pallas_call | solution.py:1247
  88.7 54.1 %feed_forward.1 = (bf16[128,1152]{1,0:T(8,128)(2,1)}, f32[128,1152]{1,0:T(8,128)}, bf16[128,1152]{1,0:T(8,128)(2,1)}, bf16[128,1152]{1,0:T(8,128)(2,1)}, f32[1,1...) custom-call(bf16[128,1152]{1,0:T(8,128)(2,1)} %normed_ref.1, ...), custom_call_target="tpu_custom_call" | custom-call | tf_op jit(solution)/shard_map/feed_forward/pallas_call | solution.py:1545
  142.8 134.6 %backward.1 = (f32[128,1152]{1,0:T(8,128)}, f32[72,576]{1,0:T(8,128)}, f32[24,576]{1,0:T(8,128)}, f32[24,576]{1,0:T(8,128)}, f32[24,128]{1,0:T(8,128)}, /*index=...) custom-call(s32[4]{0:T(128)} %docs.3, bf16[1152,128]{1,0:T(8,128)(2,1)} %get-tuple-element.56.q_ref, ...), custom_call_target="tpu_custom_call" | custom-call | flops 10000000000 | bytes 30000000 | tf_op jit(solution)/shard_map/backward/pallas_call | solution.py:789
  277.5 3.4 %finish.1 = (bf16[128,1152]{1,0:T(8,128)(2,1)}, f32[128,1152]{1,0:T(8,128)}, f32[72,576]{1,0:T(8,128)}, f32[24,576]{1,0:T(8,128)}, f32[24,576]{1,0:T(8,128)}, /*...) custom-call(bf16[128,1152]{1,0:T(8,128)(2,1)} %get-tuple-element.55.refs_0_, ...), custom_call_target="tpu_custom_call" | custom-call | tf_op jit(solution)/shard_map/finish/pallas_call | solution.py:1601
  280.9 1.4 slice_bitcast_fusion
  (3 shorter events, 0.0 us)

commit v6 on v5

--- a/solution.py
+++ b/solution.py
@@ -656,6 +656,7 @@
     tokens_ref[...] = gres_ref[...] + inv_ref[...] * (scaled - normed * mean)
 
     to_homes(0, 0)
+    to_homes(1, 3)
     share_wait(0)
     columns(colq_ref, 0, pq)
 
@@ -670,7 +671,6 @@
         return copy
 
     half_q = give_half(0, pq, 5)
-    to_homes(1, 3)
     dsum = w_total(1)
     dsend[...] = dsum.astype(dsend.dtype)
     down_copy = g_copy(4, dsend, din, mate_at)

time: 286 us -> 286 us (level)
  Pallas kernels: 276 us -> 279 us
where the time goes in v6:
time: 286 us; the launch traced here: 285 us
  Pallas kernels  279 us (98%)
  local copies, waits for them, and re-layouts  3.9 us (1%)
    pallas_call x1, Pallas kernels, backward(): pl.pallas_call(functools.partial(backward_kernel, (nctx, nf, parts, heads...  137 us
    pallas_call x1, Pallas kernels, forward(): pl.pallas_call(functools.partial(forward_kernel, (nctx, nf, parts, heads,...  84 us
    pallas_call x1, Pallas kernels, feed_forward(): pl.pallas_call(functools.partial(feed_forward_kernel, (nctx, nf)), out_sh...  54.1 us

profile of v6, /device:TPU:15, one launch (start us, length us, event | category | flops | bytes accessed | tf_op | source)
XLA Modules:
  0.0 284.7 jit_solution(11804041593355351547)
XLA Ops:
  0.7 0.7 select_reduce_fusion
  1.4 1.3 broadcast_in_dim.14.norm_attn_ref
  2.7 1.3 broadcast_in_dim.22.norm_mlp_ref
  4.0 0.8 multiply_sine_fusion
  4.7 84.0 %forward.1 = (bf16[1152,128]{1,0:T(8,128)(2,1)}, bf16[4,2,2,2,128,768]{5,4,3,2,1,0:T(8,128)(2,1)}, bf16[128,1152]{1,0:T(8,128)(2,1)}, f32[6,64,384]{2,1,0:T(8,12...) custom-call(s32[4]{0:T(128)} %docs.3, ...), custom_call_target="tpu_custom_call" | custom-call | tf_op jit(solution)/shard_map/forward/pallas_call | solution.py:1247
  88.7 54.1 %feed_forward.1 = (bf16[128,1152]{1,0:T(8,128)(2,1)}, f32[128,1152]{1,0:T(8,128)}, bf16[128,1152]{1,0:T(8,128)(2,1)}, bf16[128,1152]{1,0:T(8,128)(2,1)}, f32[1,1...) custom-call(bf16[128,1152]{1,0:T(8,128)(2,1)} %normed_ref.1, ...), custom_call_target="tpu_custom_call" | custom-call | tf_op jit(solution)/shard_map/feed_forward/pallas_call | solution.py:1545
  142.8 137.1 %backward.1 = (f32[128,1152]{1,0:T(8,128)}, f32[72,576]{1,0:T(8,128)}, f32[24,576]{1,0:T(8,128)}, f32[24,576]{1,0:T(8,128)}, f32[24,128]{1,0:T(8,128)}, /*index=...) custom-call(s32[4]{0:T(128)} %docs.3, bf16[1152,128]{1,0:T(8,128)(2,1)} %get-tuple-element.56.q_ref, ...), custom_call_target="tpu_custom_call" | custom-call | flops 10000000000 | bytes 30000000 | tf_op jit(solution)/shard_map/backward/pallas_call | solution.py:789
  280.0 3.4 %finish.1 = (bf16[128,1152]{1,0:T(8,128)(2,1)}, f32[128,1152]{1,0:T(8,128)}, f32[72,576]{1,0:T(8,128)}, f32[24,576]{1,0:T(8,128)}, f32[24,576]{1,0:T(8,128)}, /*...) custom-call(bf16[128,1152]{1,0:T(8,128)(2,1)} %get-tuple-element.55.refs_0_, ...), custom_call_target="tpu_custom_call" | custom-call | tf_op jit(solution)/shard_map/finish/pallas_call | solution.py:1601
  283.4 1.4 slice_bitcast_fusion
  (3 shorter events, 0.0 us)
